TPU v7x, 256 devices: a whole 4x4x8 slice. The times are simulated.
256 devices in a mesh: rows: 64 (over y, z, core), cols: 4 (over x).
Axes of the slice: x: 4, y: 4, z: 8, core: 2. Of those that a mesh axis runs over, the one named last changes fastest.
Arguments:
- user_factors: float32 [128, 131072], P('cols', 'rows'), may hold values from -6 to 6
- item_factors: bfloat16 [128, 524288], P('cols', 'rows'), may hold values from -0.0078125 to 0.0078125
- tile_user: int32 [4608], P('rows'), may hold values from 0 to 7
- tile_item: int32 [4608], P('rows'), may hold values from 0 to 2047, as said below
- tile_count: int32 [64], P('rows'), may hold values from 36 to 72, as said below
- tile_mask: bfloat16 [4608, 256, 256], P('rows'), may hold values from 0 to 2, as said below
Outputs:
- solution_field: float32 [128, 131072], P('cols', 'rows')
- residual: float32 [128, 131072], P('cols', 'rows')
Inputs may be any that keep to these rules, and one draw needn't show every extreme that they name: `tile_item`: item block b is held by index b // 32 of rows. Among the live slots of one index of rows at most 2 name item blocks held by one index of rows, and in every draw some index reaches 2. `tile_count`: some index of rows has all 72 slots live in every draw. `tile_mask`: each entry is zero or a strength of 0.5 or more.
All inputs are finite; a program needn't handle non-finite values.
Results may differ from a plain program's by a relative error of at most 0.0008.
Values may be sent and summed in bfloat16 or wider, within the bound.
A program may use at most 128 MiB of HBM per device.

v0:
```python
import jax
import jax.numpy as jnp
from jax import lax
from jax.sharding import PartitionSpec as P

ITERS = 2


ridge = 0.5
confidence = 40.0
highest = lax.Precision.HIGHEST


def lookup(table, wanted):
    picked = table[jnp.maximum(wanted, 0)]
    return jnp.where((wanted >= 0)[:, :, None, None], picked, jnp.zeros_like(picked))


def squares(vector):
    return lax.psum(jnp.sum(vector * vector), ("rows", "cols"))


def on_device(user_factors, item_factors, tile_user, tile_item, tile_count, tile_mask):
    tile_rows = tile_mask.shape[1]
    col_width = user_factors.shape[0]
    column = lax.axis_index("cols")
    row_devs = lax.axis_size("rows")
    tile_total = tile_user.shape[0]
    user_blocks = user_factors.shape[1] // tile_rows
    item_blocks = item_factors.shape[1] // tile_rows
    capacity = max(2, (tile_total + row_devs - 1) // row_devs)
    order = jnp.arange(tile_total, dtype=jnp.int32)
    live = (order < tile_count[0]).astype(jnp.int32)
    holder = tile_item // item_blocks
    local_block = tile_item % item_blocks
    earlier = (
        (holder[None, :] == holder[:, None])
        & (order[None, :] < order[:, None])
        & (live[None, :] > 0)
    )
    rank = jnp.sum(earlier.astype(jnp.int32), axis=1)
    slot_ids = jnp.minimum(holder * capacity + rank, row_devs * capacity - 1)
    slot_range = jnp.arange(row_devs * capacity, dtype=jnp.int32)
    hits = ((slot_ids[None, :] == slot_range[:, None]) & (live[None, :] > 0)).astype(jnp.int32)
    requests = (jnp.sum(hits * (local_block + 1)[None, :], axis=1) - 1).reshape(row_devs, capacity)
    own_full = lax.all_gather(item_factors, "cols", axis=0, tiled=True)
    own_float = own_full.astype(jnp.float32)
    own_cols = lax.dynamic_slice_in_dim(own_float, column * col_width, col_width, 0)
    gram_part = jnp.dot(own_cols, own_float.T, precision=highest)
    gram_rows = lax.psum(gram_part, "rows")
    table_full = jnp.transpose(
        own_full.reshape(own_full.shape[0], item_blocks, tile_rows), (1, 0, 2)
    )
    fetched = lax.all_to_all(
        lookup(
            table_full, lax.all_to_all(requests, "rows", split_axis=0, concat_axis=0, tiled=True)
        ),
        "rows",
        split_axis=0,
        concat_axis=0,
        tiled=True,
    )
    full_width = fetched.shape[2]
    item_tiles = fetched.reshape(row_devs * capacity, full_width, tile_rows)[slot_ids].astype(
        jnp.float32
    )
    item_cols = lax.dynamic_slice_in_dim(item_tiles, column * col_width, col_width, 1)
    masks = tile_mask * live.astype(jnp.bfloat16)[:, None, None]
    select = (tile_user[None, :] == jnp.arange(user_blocks, dtype=jnp.int32)[:, None]).astype(
        jnp.float32
    )

    def collect(terms):
        summed = jnp.einsum("bt,tcu->cbu", select, terms, precision=highest)
        return summed.reshape(col_width, user_blocks * tile_rows)

    right_side = (1.0 + confidence) * collect(
        jnp.einsum("tui,tci->tcu", masks.astype(jnp.float32), item_cols, precision=highest)
    )

    def apply_op(dirs):
        dirs_full = lax.all_gather(dirs, "cols", axis=0, tiled=True)
        dir_tiles = dirs_full.reshape(full_width, user_blocks, tile_rows)[:, tile_user]
        scores = jnp.einsum(
            "ktu,tki->tui", dir_tiles, item_tiles, precision=highest
        ) * masks.astype(jnp.float32)
        sparse = collect(jnp.einsum("tui,tci->tcu", scores, item_cols, precision=highest))
        return jnp.dot(gram_rows, dirs_full, precision=highest) + ridge * dirs + confidence * sparse

    solution_field = user_factors
    residual = right_side - apply_op(user_factors)
    direction = residual
    norm_now = squares(residual)
    for iteration in range(ITERS):
        image = apply_op(direction)
        alpha = norm_now / lax.psum(jnp.sum(direction * image), ("rows", "cols"))
        solution_field = solution_field + alpha * direction
        residual = residual - alpha * image
        norm_next = squares(residual)
        direction = residual + norm_next / norm_now * direction
        norm_now = norm_next
    return (solution_field, residual)


def solution(mesh):
    return jax.shard_map(
        on_device,
        mesh=mesh,
        in_specs=(
            P("cols", "rows"),
            P("cols", "rows"),
            P("rows"),
            P("rows"),
            P("rows"),
            P("rows", None, None),
        ),
        out_specs=(P("cols", "rows"), P("cols", "rows")),
        check_vma=False,
    )
```

profile of v0, /device:TPU:1, one launch (start us, length us, event | category | flops | bytes accessed | tf_op | source)
XLA Modules:
  0.0 919.8 jit_solution(7542263093620790036)
XLA Ops:
  7.2 0.7 all-gather.5.cloned.1.call-update
  8.6 0.7 and_select_fusion.1
  9.2 0.2 convert_reduce_fusion
  9.5 0.1 sub.23
  9.7 22.2 %all_to_all.11 = s32[64,1,2]{2,1,0:T(1,128)S(1)} all-to-all(s32[64,1,2]{2,1,0:T(1,128)S(1)} %bitcast.71), channel_id=1, replica_groups=mesh['rows'=64,'cols'=4] {'rows'}, dimensions={0} | all-to-all | bytes 1024 | tf_op jit(solution)/shard_map/all_to_all | solution.py:56
  32.0 0.1 reshape.91
  32.3 0.1 copy.47
  32.4 14.6 %all-gather.5.cloned.1.call-done = bf16[128,8192]{1,0:T(8,128)(2,1)} async-done(((bf16[32,8192]{1,0:T(8,128)(2,1)}), bf16[128,8192]{1,0:T(8,128)(2,1)}) %all-gather.5.cloned.1.call-update) | async-done | bytes 2097168 | tf_op jit(solution)/shard_map/all_gather | solution.py:46
  47.0 4.1 copy.48
  51.1 3.3 copy.49
  54.4 6.4 gather_fusion
  60.8 7.2 broadcast_select_fusion
  68.1 11.0 %all-to-all-start.1 = ((bf16[64,2,128,256]{3,2,1,0:T(8,128)(2,1)}), bf16[64,2,128,256]{3,2,1,0:T(8,128)(2,1)}, u32[]{:S(2)}, u32[]{:S(2)}) async-start(bf16[64,2,128,256]{3,2,1,0:T(8,128)(2,1)} %broadcast_select_fusion), calls=%async_computation.1 | async-start | bytes 16777216 | tf_op jit(solution)/shard_map/all_to_all | solution.py:54
  79.1 0.7 all-gather.7.cloned.1.call-update
  79.9 27.1 %all-gather.7.cloned.1.call-done = f32[128,2048]{1,0:T(8,128)} async-done(((f32[32,2048]{1,0:T(8,128)}), f32[128,2048]{1,0:T(8,128)}) %all-gather.7.cloned.1.call-update) | async-done | bytes 1048592 | tf_op jit(solution)/shard_map/all_gather | solution.py:82
  107.0 1.5 copy.51
  108.6 0.3 copy.52
  108.9 4.9 gather_fusion.2
  113.8 0.8 fusion.46
  114.6 381.4 %psum.35 = f32[32,128]{1,0:T(8,128)S(1)} all-reduce(f32[32,128]{1,0:T(8,128)S(1)} %fusion.46), channel_id=1, replica_groups=mesh['rows'=64,'cols'=4] {'rows'}, use_global_device_ids=true, to_apply=%region_2.3 | all-reduce | flops 4096 | bytes 32768 | tf_op jit(solution)/shard_map/psum | solution.py:50
  496.0 8.9 gather_fusion.1
  504.9 7.1 fusion.12
  512.0 2.2 fusion.30
  514.2 0.8 copy.66
  515.0 14.4 %fusion.7 = f32[72,256,256]{2,1,0:T(8,128)} fusion(bf16[72,128,256]{2,1,0:T(8,128)(2,1)S(1)} %copy-done, f32[72,128,256]{2,1,0:T(8,128)} %gather_fusion.2), kind=kOutput, calls=%fused_computation.15 | convolution fusion | flops 7247757312 | bytes 33030144 | tf_op jit(solution)/shard_map/ktu,tki->tui/dot_general | solution.py:84
  529.4 15.8 %fusion = f32[72,32,256]{2,1,0:T(8,128)S(1)} fusion(f32[72,256,256]{2,1,0:T(8,128)} %fusion.7, bf16[72,256,256]{2,1,0:T(8,128)(2,1)} %param.11, bf16[72]{0:T(256)(128)(2,1)S(1)} %fusion.61, bf16[72,128,256]{2,1,0:T(8,128)(2,1)} %gather_fusion.1, s32[]{:T(128)S(6)} %select_n.33), kind=kOutput, calls=%fused_computation.8 | convolution fusion | flops 1826095104 | bytes 31850644 | tf_op jit(solution)/shard_map/tui,tci->tcu/dot_general | solution.py:87
  545.2 2.2 fusion.33
  547.5 2.4 fusion.29
  550.0 23.1 %all-gather.9.cloned.1.call-done = f32[128,2048]{1,0:T(8,128)} async-done(((f32[32,2048]{1,0:T(8,128)}), f32[128,2048]{1,0:T(8,128)}) %all-gather.9.cloned.1.call-update) | async-done | bytes 1048592 | tf_op jit(solution)/shard_map/all_gather | solution.py:82
  573.1 1.3 copy.89
  574.4 4.9 gather_fusion.3
  579.3 15.4 %fusion.5 = f32[72,256,256]{2,1,0:T(8,128)} fusion(bf16[72,128,256]{2,1,0:T(8,128)(2,1)} %gather_fusion.1, f32[72,128,256]{2,1,0:T(8,128)} %gather_fusion.3), kind=kOutput, calls=%fused_computation.13 | convolution fusion | flops 7247757312 | bytes 33030144 | tf_op jit(solution)/shard_map/ktu,tki->tui/dot_general | solution.py:84
  594.7 15.6 %fusion.1 = f32[72,32,256]{2,1,0:T(8,128)S(1)} fusion(f32[72,256,256]{2,1,0:T(8,128)} %fusion.5, bf16[72,256,256]{2,1,0:T(8,128)(2,1)} %param.11, bf16[72]{0:T(256)(128)(2,1)S(1)} %fusion.61, bf16[72,128,256]{2,1,0:T(8,128)(2,1)} %gather_fusion.1, s32[]{:T(128)S(6)} %select_n.33), kind=kOutput, calls=%fused_computation.9 | convolution fusion | flops 1826095104 | bytes 31850644 | tf_op jit(solution)/shard_map/tui,tci->tcu/dot_general | solution.py:87
  610.4 2.2 fusion.36
  612.6 2.5 multiply_reduce_fusion.2
  615.2 76.9 %all-reduce = (f32[]{:T(128)}, f32[]{:T(128)}) all-reduce(f32[]{:T(128)} %get-tuple-element.3, f32[]{:T(128)} %get-tuple-element.2), channel_id=1, replica_groups=mesh['rows'=64,'cols'=4] {'rows','cols'}, use_global_device_ids=true, to_apply=%region_4.5 | all-reduce | flops 2 | bytes 16 | tf_op jit(solution)/shard_map/psum | solution.py:20
  693.4 0.7 multiply_reduce_fusion.1
  694.1 73.7 %psum.38 = f32[]{:T(128)} all-reduce(f32[]{:T(128)} %multiply_reduce_fusion.1), channel_id=1, replica_groups=mesh['rows'=64,'cols'=4] {'rows','cols'}, use_global_device_ids=true, to_apply=%region_8.9 | all-reduce | flops 1 | bytes 8 | tf_op jit(solution)/shard_map/psum | solution.py:20
  769.2 0.7 multiply_add_fusion.1
  769.9 22.0 %all-gather.11.cloned.1.call-done = f32[128,2048]{1,0:T(8,128)} async-done(((f32[32,2048]{1,0:T(8,128)}), f32[128,2048]{1,0:T(8,128)}) %all-gather.11.cloned.1.call-update) | async-done | bytes 1048592 | tf_op jit(solution)/shard_map/all_gather | solution.py:82
  791.9 1.3 copy.88
  793.3 4.9 gather_fusion.4
  798.1 15.2 %fusion.3 = f32[72,256,256]{2,1,0:T(8,128)} fusion(bf16[72,128,256]{2,1,0:T(8,128)(2,1)} %gather_fusion.1, f32[72,128,256]{2,1,0:T(8,128)} %gather_fusion.4), kind=kOutput, calls=%fused_computation.11 | convolution fusion | flops 7247757312 | bytes 33030144 | tf_op jit(solution)/shard_map/ktu,tki->tui/dot_general | solution.py:84
  813.3 15.7 %fusion.2 = f32[72,32,256]{2,1,0:T(8,128)S(1)} fusion(f32[72,256,256]{2,1,0:T(8,128)} %fusion.3, bf16[72,256,256]{2,1,0:T(8,128)(2,1)} %param.11, bf16[72]{0:T(256)(128)(2,1)S(1)} %fusion.61, bf16[72,128,256]{2,1,0:T(8,128)(2,1)} %gather_fusion.1, s32[]{:T(128)S(6)} %select_n.33), kind=kOutput, calls=%fused_computation.10 | convolution fusion | flops 1826095104 | bytes 31850644 | tf_op jit(solution)/shard_map/tui,tci->tcu/dot_general | solution.py:87
  829.0 2.2 fusion.39
  831.3 2.5 multiply_reduce_fusion
  833.8 76.7 %psum.39 = f32[]{:T(128)} all-reduce(f32[]{:T(128)} %get-tuple-element.13), channel_id=1, replica_groups=mesh['rows'=64,'cols'=4] {'rows','cols'}, use_global_device_ids=true, to_apply=%region_10.11 | all-reduce | flops 1 | bytes 8 | tf_op jit(solution)/shard_map/psum | solution.py:96
  911.9 0.9 multiply_subtract_fusion
  (36 shorter events, 0.9 us)
Async XLA Ops:
  7.2 39.8 %all-gather.5.cloned.1.call-start = ((), (), s32[]{:S(2)}) async-start(), calls=%async_computation.2 | async-start | bytes 2621440 | tf_op jit(solution)/shard_map/all_gather | solution.py:46
  68.1 11.8 %copy-start.6 = (s32[72]{0:T(128)S(1)}, s32[72]{0:T(128)}, u32[]{:S(2)}) copy-start(s32[72]{0:T(128)} %param.8) | copy-start | bytes 868
  68.1 427.9 %all-to-all-start.1 = ((bf16[64,2,128,256]{3,2,1,0:T(8,128)(2,1)}), bf16[64,2,128,256]{3,2,1,0:T(8,128)(2,1)}, u32[]{:S(2)}, u32[]{:S(2)}) async-start(bf16[64,2,128,256]{3,2,1,0:T(8,128)(2,1)} %broadcast_select_fusion), calls=%async_computation.1 | async-start | bytes 16777216 | tf_op jit(solution)/shard_map/all_to_all | solution.py:54
  79.1 28.0 %all-gather.7.cloned.1.call-start = ((), (), s32[]{:S(2)}) async-start(), calls=%async_computation.3 | async-start | bytes 1310720 | tf_op jit(solution)/shard_map/all_gather | solution.py:82
  79.8 493.3 %all-gather.9.cloned.1.call-start = ((), (), s32[]{:S(2)}) async-start(), calls=%async_computation.4 | async-start | bytes 1310720 | tf_op jit(solution)/shard_map/all_gather | solution.py:82
  108.9 4.9 copy-start.2
  504.9 10.1 %copy-start = (bf16[72,128,256]{2,1,0:T(8,128)(2,1)S(1)}, bf16[72,128,256]{2,1,0:T(8,128)(2,1)}, u32[]{:S(2)}) copy-start(bf16[72,128,256]{2,1,0:T(8,128)(2,1)} %gather_fusion.1) | copy-start | bytes 14155780
  529.4 18.1 %copy-start.3 = (f32[128,2048]{1,0:T(8,128)S(1)}, f32[128,2048]{1,0:T(8,128)}, u32[]{:S(2)}) copy-start(f32[128,2048]{1,0:T(8,128)} %all-gather.7.cloned.1.call-done) | copy-start | bytes 3145732
  550.0 242.0 %all-gather.11.cloned.1.call-start = ((), (), s32[]{:S(2)}) async-start(), calls=%async_computation.5 | async-start | bytes 1310720 | tf_op jit(solution)/shard_map/all_gather | solution.py:82
  594.7 17.9 %copy-start.1 = (f32[32,2048]{1,0:T(8,128)S(1)}, f32[32,2048]{1,0:T(8,128)}, u32[]{:S(2)}) copy-start(f32[32,2048]{1,0:T(8,128)} %fusion.29) | copy-start | bytes 786436
  813.3 17.9 %copy-start.4 = (f32[32,2048]{1,0:T(8,128)S(1)}, f32[32,2048]{1,0:T(8,128)}, u32[]{:S(2)}) copy-start(f32[32,2048]{1,0:T(8,128)} %multiply_add_fusion.1) | copy-start | bytes 786436
  813.3 98.6 %copy-start.5 = (f32[32,2048]{1,0:T(8,128)S(1)}, f32[32,2048]{1,0:T(8,128)}, u32[]{:S(2)}) copy-start(f32[32,2048]{1,0:T(8,128)} %param.6) | copy-start | bytes 786436
Sparse Core Ops, SparseCore 0:
  9.8 37.1 all-gather.4
  81.7 25.2 all-gather.6
  550.1 22.9 all-gather.8
  770.0 21.8 all-gather.10
where the time goes:
time: 926 us; the launch traced here: 920 us
  blocking collectives  631 us (68%)
  matrix products  116 us (13%)
  waiting for transfers between devices  88.2 us (10%)
  local copies, waits for them, and re-layouts  43.4 us (5%)
  between operations  19.2 us (2%)
  starting transfers between devices  11.2 us (1%)
  other arithmetic  10.6 us (1%)
    psum x1, blocking collectives, on_device(): gram_rows = lax.psum(gram_part, 'rows')  381 us
    psum x2, blocking collectives, squares(): return lax.psum(jnp.sum(vector * vector), ('rows', 'cols'))  151 us
    psum x1, blocking collectives, on_device(): alpha = norm_now / lax.psum(jnp.sum(direction * image), ('rows', 'cols'))  76.7 us
    all_gather x3, waiting for transfers between devices, apply_op(): dirs_full = lax.all_gather(dirs, 'cols', axis=0, tiled=True)  72.2 us
    dot_general x3, matrix products, apply_op(): jnp.einsum('tui,tci->tcu', scores, item_cols, precision=highest)  47.1 us
    dot_general x3, matrix products, apply_op(): jnp.einsum('ktu,tki->tui', dir_tiles, item_tiles, precision=highest)  45 us
    all_to_all x1, blocking collectives, on_device(): lax.all_to_all(requests, 'rows', split_axis=0, concat_axis=0, tiled=True)  22.2 us
  transfers between devices with their start and end apart: 5, of which 4 were waited for; matrix products, arithmetic and copies ran while one was open for 1% of the time, Pallas kernels for 0%

commit v1 on v0

v1 whole, which is shorter than its diff:
```python
import jax
import jax.numpy as jnp
from jax import lax
from jax.experimental import pallas as pl
from jax.experimental.pallas import tpu as pltpu
from jax.sharding import PartitionSpec as P

RIDGE = 0.5
CONFIDENCE = 40.0
HIGHEST = lax.Precision.HIGHEST
MESH = pl.DeviceIdType.MESH
F32 = jnp.float32
BF16 = jnp.bfloat16
Y_CHIPS = 4
GROUP = 16
VMEM_BYTES = 48 * 1024 * 1024


def half_lanes(shape):
    return lax.broadcasted_iota(jnp.int32, shape, 1) < 64


def cg_kernel(
    perm_ref, user_ref, keep_ref, live_ref, last_ref, has_ref,
    users_ref, items_ref, tiles_ref, mask_ref,
    solution_ref, residual_ref,
    masks, users_send, users_recv, items_recv, gram_part, gram_recv, gram_piece, gram_all, gram,
    sums_send, sums_recv, halves, terms, state_x, state_r, state_q, image, out_send, out_recv,
    mask_sem, x_send_sems, x_recv_sems, i_send_sems, i_recv_sems, g_send_sems, g_recv_sems,
    s_send_sems, s_recv_sems, o_send_sems, o_recv_sems,
):
    row = lax.axis_index("rows")
    col = lax.axis_index("cols")
    n_cols = lax.axis_size("cols")
    own_a = lax.rem(row, GROUP)
    own_y = lax.div(row, GROUP)
    own_b = col * Y_CHIPS + own_y
    tile_total, own_users, tile_cols = masks.shape
    col_width = users_ref.shape[0]
    blocks = halves.shape[0]
    item_quarter = items_recv.shape[1]

    def peer_a(j):
        return (own_y * GROUP + j, col)

    def peer_b(j):
        return (lax.rem(j, Y_CHIPS) * GROUP + own_a, lax.div(j, Y_CHIPS))

    def others(own, count, body):
        def step(i, carry):
            body(lax.rem(own + i, count))
            return carry

        lax.fori_loop(1, count, step, 0)

    mask_copy = pltpu.make_async_copy(
        mask_ref.at[:, pl.ds(pl.multiple_of(col * own_users, own_users), own_users), :], masks, mask_sem
    )
    mask_copy.start()

    barrier = pltpu.get_barrier_semaphore()
    others(own_a, GROUP, lambda j: pl.semaphore_signal(barrier, inc=1, device_id=peer_a(j), device_id_type=MESH))
    others(own_b, GROUP, lambda j: pl.semaphore_signal(barrier, inc=1, device_id=peer_b(j), device_id_type=MESH))

    for dest in range(n_cols):
        for pair in range(blocks // 2):
            first = users_ref[:, pl.ds((2 * pair) * 256 + (dest // 2) * 128, 128)]
            second = users_ref[:, pl.ds((2 * pair + 1) * 256 + (dest // 2) * 128, 128)]
            low = half_lanes(first.shape)
            if dest % 2 == 0:
                joined = jnp.where(low, first, pltpu.roll(second, 64, 1))
            else:
                joined = jnp.where(low, pltpu.roll(first, 64, 1), second)
            users_send[dest, :, pl.ds(pair * 128, 128)] = joined
    pl.semaphore_wait(barrier, 2 * (GROUP - 1))

    def item_copy(j):
        return pltpu.make_async_remote_copy(
            src_ref=items_ref.at[:, pl.ds(pl.multiple_of(j * item_quarter, item_quarter), item_quarter)],
            dst_ref=items_recv.at[pl.ds(pl.multiple_of(col * col_width, col_width), col_width)],
            send_sem=i_send_sems.at[j], recv_sem=i_recv_sems.at[col],
            device_id=(row, j), device_id_type=MESH,
        )

    def item_arrival(j):
        return pltpu.make_async_remote_copy(
            src_ref=items_ref.at[:, pl.ds(pl.multiple_of(j * item_quarter, item_quarter), item_quarter)],
            dst_ref=items_recv.at[pl.ds(pl.multiple_of(j * col_width, col_width), col_width)],
            send_sem=i_send_sems.at[j], recv_sem=i_recv_sems.at[j],
            device_id=(row, j), device_id_type=MESH,
        )

    def user_copy(j):
        return pltpu.make_async_remote_copy(
            src_ref=users_send.at[j], dst_ref=users_recv.at[pl.ds(pl.multiple_of(col * col_width, col_width), col_width)],
            send_sem=x_send_sems.at[j], recv_sem=x_recv_sems.at[col],
            device_id=(row, j), device_id_type=MESH,
        )

    def user_arrival(j):
        return pltpu.make_async_remote_copy(
            src_ref=users_send.at[j], dst_ref=users_recv.at[pl.ds(pl.multiple_of(j * col_width, col_width), col_width)],
            send_sem=x_send_sems.at[j], recv_sem=x_recv_sems.at[j],
            device_id=(row, j), device_id_type=MESH,
        )

    others(col, n_cols, lambda j: item_copy(j).start())
    others(col, n_cols, lambda j: user_copy(j).start())
    own_rows = pl.ds(pl.multiple_of(col * col_width, col_width), col_width)
    items_recv[own_rows, :] = items_ref[:, pl.ds(pl.multiple_of(col * item_quarter, item_quarter), item_quarter)]
    users_recv[own_rows, :] = users_send[col]

    others(col, n_cols, lambda j: item_arrival(j).wait_recv())
    table = items_recv[...]
    gram_part[...] = lax.dot_general(
        table, table, (((1,), (1,)), ((), ())), preferred_element_type=F32
    ).reshape(gram_part.shape)

    def gram_copy(stage, src, dst, slot, j, peer):
        return pltpu.make_async_remote_copy(
            src_ref=src, dst_ref=dst, send_sem=g_send_sems.at[stage, j], recv_sem=g_recv_sems.at[stage, slot],
            device_id=peer(j), device_id_type=MESH,
        )

    def gram_first(j, slot):
        return gram_copy(0, gram_part.at[j], gram_recv.at[slot], slot, j, peer_a)

    def gram_second(j, slot):
        return gram_copy(1, gram_piece, gram_all.at[slot], slot, j, peer_b)

    def gram_third(j, slot):
        return gram_copy(2, gram.at[own_a], gram.at[slot], slot, j, peer_a)

    others(own_a, GROUP, lambda j: gram_first(j, own_a).start())
    gram_recv[own_a] = gram_part[own_a]
    others(own_a, GROUP, lambda j: gram_first(j, j).wait_recv())
    gram_piece[...] = jnp.sum(gram_recv[...], axis=0)
    others(own_b, GROUP, lambda j: gram_second(j, own_b).start())
    gram_all[own_b] = gram_piece[...]
    others(own_b, GROUP, lambda j: gram_second(j, j).wait_recv())
    gram[own_a] = jnp.sum(gram_all[...], axis=0)
    others(own_a, GROUP, lambda j: gram_third(j, own_a).start())

    others(col, n_cols, lambda j: user_arrival(j).wait_recv())
    state_x[...] = users_recv[...].T
    mask_copy.wait()

    def sparse_part(vectors, first_time):
        high = vectors.astype(BF16)
        low = (vectors - high.astype(F32)).astype(BF16)
        halves[:, :, :128] = high.reshape(blocks, own_users, 128)
        halves[:, :, 128:] = low.reshape(blocks, own_users, 128)

        def step(s, running):
            item = tiles_ref[s]
            scores = jnp.dot(
                halves[user_ref[s]], jnp.concatenate([item, item], axis=0), preferred_element_type=F32
            )
            mask = masks[perm_ref[s]].astype(F32) * live_ref[s]
            if first_time:
                strengths = mask * ((1.0 + CONFIDENCE) - CONFIDENCE * scores)
            else:
                strengths = mask * scores
            s_high = strengths.astype(BF16)
            s_low = (strengths - s_high.astype(F32)).astype(BF16)
            both = lax.dot_general(
                jnp.concatenate([s_high, s_low], axis=0), item, (((1,), (1,)), ((), ())),
                preferred_element_type=F32,
            )
            running = both[:own_users] + both[own_users:] + keep_ref[s] * running
            terms[s] = running
            return running

        lax.fori_loop(0, tile_total, step, jnp.zeros((own_users, 128), F32), unroll=4)
        return jnp.concatenate([terms[last_ref[b]] * has_ref[b] for b in range(blocks)], axis=0)

    def dense_part(vectors):
        return (
            jnp.dot(vectors, gram[...].reshape(128, 128), precision=HIGHEST, preferred_element_type=F32)
            + RIDGE * vectors
        )

    def all_sums(round_index, products):
        rows = [jnp.sum(p, axis=0, keepdims=True) for p in products]
        rows.append(jnp.zeros((8 - len(rows), 128), F32))
        total = jnp.concatenate(rows, axis=0)
        for stage, (peer, own) in enumerate(((peer_a, own_a), (peer_b, own_b))):
            at = 2 * round_index + stage

            def copy(j, slot, at=at, peer=peer):
                return pltpu.make_async_remote_copy(
                    src_ref=sums_send.at[at], dst_ref=sums_recv.at[at, slot],
                    send_sem=s_send_sems.at[at, j], recv_sem=s_recv_sems.at[at, slot],
                    device_id=peer(j), device_id_type=MESH,
                )

            sums_send[at] = total
            others(own, GROUP, lambda j: copy(j, own).start())
            sums_recv[at, own] = total
            others(own, GROUP, lambda j: copy(j, j).wait_recv())
            total = jnp.sum(sums_recv[at], axis=0)
            others(own, GROUP, lambda j: copy(j, j).wait_send())
        total = jnp.sum(total, axis=1, keepdims=True)
        return [total[i : i + 1, :] for i in range(len(products))]

    start = sparse_part(state_x[...], True)
    others(own_a, GROUP, lambda j: gram_third(j, j).wait_recv())
    state_r[...] = start - dense_part(state_x[...])

    image[...] = dense_part(state_r[...]) + CONFIDENCE * sparse_part(state_r[...], False)
    norm_0, curve_0 = all_sums(0, [state_r[...] * state_r[...], state_r[...] * image[...]])
    alpha_0 = norm_0 / curve_0
    state_q[...] = state_r[...]
    state_x[...] = state_x[...] + alpha_0 * state_r[...]
    state_r[...] = state_r[...] - alpha_0 * image[...]

    image_r = dense_part(state_r[...]) + CONFIDENCE * sparse_part(state_r[...], False)
    norm_1, curve_rr, curve_rd, curve_dr = all_sums(
        1,
        [
            state_r[...] * state_r[...],
            state_r[...] * image_r,
            state_r[...] * image[...],
            state_q[...] * image_r,
        ],
    )
    beta = norm_1 / norm_0
    alpha_1 = norm_1 / (curve_rr + beta * (curve_rd + curve_dr) + beta * beta * curve_0)
    out_x = state_x[...] + alpha_1 * (state_r[...] + beta * state_q[...])
    out_r = state_r[...] - alpha_1 * (image_r + beta * image[...])

    out_send[0] = out_x.T.reshape(n_cols, col_width, blocks * own_users)
    out_send[1] = out_r.T.reshape(n_cols, col_width, blocks * own_users)

    def out_copy(j, slot):
        return pltpu.make_async_remote_copy(
            src_ref=out_send.at[:, j], dst_ref=out_recv.at[slot],
            send_sem=o_send_sems.at[j], recv_sem=o_recv_sems.at[slot],
            device_id=(row, j), device_id_type=MESH,
        )

    others(col, n_cols, lambda j: out_copy(j, col).start())
    out_recv[col] = out_send[:, col]
    others(col, n_cols, lambda j: out_copy(j, j).wait_recv())
    for which, out_ref in enumerate((solution_ref, residual_ref)):
        for block in range(blocks):
            lanes = pl.ds((block // 2) * 128, 128)
            for side in range(n_cols // 2):
                first = out_recv[2 * side, which, :, lanes]
                second = out_recv[2 * side + 1, which, :, lanes]
                low = half_lanes(first.shape)
                if block % 2 == 0:
                    joined = jnp.where(low, first, pltpu.roll(second, 64, 1))
                else:
                    joined = jnp.where(low, pltpu.roll(first, 64, 1), second)
                out_ref[:, pl.ds(block * 256 + side * 128, 128)] = joined

    others(col, n_cols, lambda j: item_copy(j).wait_send())
    others(col, n_cols, lambda j: user_copy(j).wait_send())
    others(own_a, GROUP, lambda j: gram_first(j, own_a).wait_send())
    others(own_b, GROUP, lambda j: gram_second(j, own_b).wait_send())
    others(own_a, GROUP, lambda j: gram_third(j, own_a).wait_send())
    others(col, n_cols, lambda j: out_copy(j, col).wait_send())


def conjugate(tables, user_factors, item_factors, tiles, tile_mask, n_cols):
    col_width, users = user_factors.shape
    slots, width, tile_cols = tiles.shape
    tile_rows = tile_mask.shape[1]
    blocks = users // tile_rows
    own_users = tile_rows // n_cols
    mine = blocks * own_users
    item_quarter = item_factors.shape[1] // n_cols
    vmem = pl.BlockSpec(memory_space=pltpu.VMEM)
    smem = pl.BlockSpec(memory_space=pltpu.SMEM)
    piece = width // GROUP
    out = jax.ShapeDtypeStruct((col_width, users), F32)
    return pl.pallas_call(
        cg_kernel,
        out_shape=(out, out),
        in_specs=[smem] * 6 + [vmem] * 3 + [pl.BlockSpec(memory_space=pl.ANY)],
        out_specs=(vmem, vmem),
        scratch_shapes=[
            pltpu.VMEM((slots, own_users, tile_cols), BF16),
            pltpu.VMEM((n_cols, col_width, mine), F32),
            pltpu.VMEM((width, mine), F32),
            pltpu.VMEM((width, item_quarter), BF16),
            pltpu.VMEM((GROUP, piece, width), F32),
            pltpu.VMEM((GROUP, piece, width), F32),
            pltpu.VMEM((piece, width), F32),
            pltpu.VMEM((GROUP, piece, width), F32),
            pltpu.VMEM((GROUP, piece, width), F32),
            pltpu.VMEM((4, 8, 128), F32),
            pltpu.VMEM((4, GROUP, 8, 128), F32),
            pltpu.VMEM((blocks, own_users, 2 * width), BF16),
            pltpu.VMEM((slots, own_users, width), F32),
            pltpu.VMEM((mine, width), F32),
            pltpu.VMEM((mine, width), F32),
            pltpu.VMEM((mine, width), F32),
            pltpu.VMEM((mine, width), F32),
            pltpu.VMEM((2, n_cols, col_width, mine), F32),
            pltpu.VMEM((n_cols, 2, col_width, mine), F32),
            pltpu.SemaphoreType.DMA,
            pltpu.SemaphoreType.DMA((n_cols,)),
            pltpu.SemaphoreType.DMA((n_cols,)),
            pltpu.SemaphoreType.DMA((n_cols,)),
            pltpu.SemaphoreType.DMA((n_cols,)),
            pltpu.SemaphoreType.DMA((3, GROUP)),
            pltpu.SemaphoreType.DMA((3, GROUP)),
            pltpu.SemaphoreType.DMA((4, GROUP)),
            pltpu.SemaphoreType.DMA((4, GROUP)),
            pltpu.SemaphoreType.DMA((n_cols,)),
            pltpu.SemaphoreType.DMA((n_cols,)),
        ],
        compiler_params=pltpu.CompilerParams(
            collective_id=0, has_side_effects=True, vmem_limit_bytes=VMEM_BYTES
        ),
    )(*tables, user_factors, item_factors, tiles, tile_mask)


def on_device(user_factors, item_factors, tile_user, tile_item, tile_count, tile_mask):
    n_rows, n_cols = lax.axis_size("rows"), lax.axis_size("cols")
    col_width = item_factors.shape[0]
    tile_rows = tile_mask.shape[1]
    slots = tile_user.shape[0]
    blocks = user_factors.shape[1] // tile_rows
    item_blocks = item_factors.shape[1] // tile_rows
    capacity = max(2, (slots + n_rows - 1) // n_rows)

    order = jnp.arange(slots, dtype=jnp.int32)
    live = order < tile_count[0]
    key = jnp.where(live, tile_user, blocks) * slots + order
    place = jnp.sum((key[None, :] < key[:, None]).astype(jnp.int32), axis=1)
    chosen = (place[None, :] == order[:, None]).astype(jnp.int32)
    perm = jnp.sum(chosen * order[None, :], axis=1)
    user = jnp.sum(chosen * tile_user[None, :], axis=1)
    live_sorted = live.astype(F32)
    keep = jnp.concatenate([jnp.zeros((1,), F32), (user[1:] == user[:-1]).astype(F32)])
    per_block = (user[None, :] == jnp.arange(blocks, dtype=jnp.int32)[:, None]) & live[None, :]
    has = jnp.any(per_block, axis=1).astype(F32)
    last = jnp.max(jnp.where(per_block, order[None, :], 0), axis=1)

    holder = tile_item // item_blocks
    earlier = (holder[None, :] == holder[:, None]) & (order[None, :] < order[:, None]) & live[None, :]
    rank = jnp.sum(earlier.astype(jnp.int32), axis=1)
    slot_ids = jnp.minimum(holder * capacity + rank, n_rows * capacity - 1)
    slot_range = jnp.arange(n_rows * capacity, dtype=jnp.int32)
    hits = ((slot_ids[None, :] == slot_range[:, None]) & live[None, :]).astype(jnp.int32)
    requests = jnp.sum(hits * (tile_item % item_blocks)[None, :], axis=1).reshape(n_rows, capacity)
    wanted = lax.all_to_all(requests, "rows", split_axis=0, concat_axis=0, tiled=True)
    shards = jnp.transpose(item_factors.reshape(col_width, item_blocks, tile_rows), (1, 0, 2))
    fetched = lax.all_to_all(shards[wanted], "rows", split_axis=0, concat_axis=0, tiled=True)
    slot_sorted = jnp.sum(chosen * slot_ids[None, :], axis=1)
    picked = fetched.reshape(n_rows * capacity, col_width, tile_rows)[slot_sorted]
    tiles = lax.all_gather(picked, "cols", axis=1, tiled=True)
    return conjugate(
        (perm, user, keep, live_sorted, last, has), user_factors, item_factors, tiles, tile_mask, n_cols
    )


def solution(mesh):
    return jax.shard_map(
        on_device,
        mesh=mesh,
        in_specs=(
            P("cols", "rows"),
            P("cols", "rows"),
            P("rows"),
            P("rows"),
            P("rows"),
            P("rows", None, None),
        ),
        out_specs=(P("cols", "rows"), P("cols", "rows")),
        check_vma=False,
    )
```

time: 926 us -> 237 us (0.26)
  blocking collectives: 631 us -> 0 us
  matrix products: 116 us -> 0 us
  Pallas kernels: 0 us -> 81.6 us
  local copies, waits for them, and re-layouts: 43.4 us -> 9.78 us
  waiting for transfers between devices: 88.2 us -> 110 us
    psum x4 -> x0, blocking collectives: 609 us -> none  [the longest x1 381 us: on_device(): gram_rows = lax.psum(gram_part, 'rows')]
    dot_general x15 -> x0, matrix products: 116 us -> none  [the longest x3 47.1 us: apply_op(): jnp.einsum('tui,tci->tcu', scores, item_cols, precision=highest)]
    pallas_call x0 -> x1, Pallas kernels: none -> 81.6 us  [conjugate(): pl.pallas_call(cg_kernel, out_shape=(out, out), in_specs=[smem] * 6 + [vm...]
    all_to_all x1 -> x2, waiting for transfers between devices: 0.01 us -> 59 us  [the longest x1 50.9 us: on_device(): lax.all_to_all(shards[wanted], 'rows', split_axis=0, concat_axis=0, tiled...]
    all_gather x4 -> x1, waiting for transfers between devices: 86.8 us -> 51.3 us  [on_device(): tiles = lax.all_gather(picked, 'cols', axis=1, tiled=True)]
    gather x5 -> x2, local copies, waits for them, and re-layouts: 30 us -> 3.84 us  [the longest x1 2.03 us: on_device(): shards[wanted]]
    all_to_all x1 -> x0, blocking collectives: 22.2 us -> none  [on_device(): lax.all_to_all(requests, 'rows', split_axis=0, concat_axis=0, tiled=True)]
  transfers between devices with their start and end apart: 5 -> 3, of which waited for: 4 -> 3; matrix products, arithmetic and copies ran while one was open for 1% -> 1% of each run, Pallas kernels for 0% -> 0%
where the time goes in v1:
time: 237 us; the launch traced here: 236 us
  waiting for transfers between devices  110 us (46%)
  Pallas kernels  81.6 us (34%)
  starting transfers between devices  18.1 us (8%)
  between operations  14.8 us (6%)
  local copies, waits for them, and re-layouts  9.78 us (4%)
    pallas_call x1, Pallas kernels, conjugate(): pl.pallas_call(cg_kernel, out_shape=(out, out), in_specs=[smem] * 6 + [vm...  81.6 us
    all_gather x1, waiting for transfers between devices, on_device(): tiles = lax.all_gather(picked, 'cols', axis=1, tiled=True)  51.3 us
    all_to_all x1, waiting for transfers between devices, on_device(): lax.all_to_all(shards[wanted], 'rows', split_axis=0, concat_axis=0, tiled...  50.9 us
    all_to_all x1, starting transfers between devices, on_device(): lax.all_to_all(requests, 'rows', split_axis=0, concat_axis=0, tiled=True)  13.2 us
    all_to_all x1, waiting for transfers between devices, on_device(): lax.all_to_all(requests, 'rows', split_axis=0, concat_axis=0, tiled=True)  8.11 us
    all_to_all x1, starting transfers between devices, on_device(): lax.all_to_all(shards[wanted], 'rows', split_axis=0, concat_axis=0, tiled...  4.92 us
  transfers between devices with their start and end apart: 3, of which 3 were waited for; matrix products, arithmetic and copies ran while one was open for 1% of the time, Pallas kernels for 0%

profile of v1, /device:TPU:1, one launch (start us, length us, event | category | flops | bytes accessed | tf_op | source)
XLA Modules:
  0.0 236.4 jit_solution(3152372317052210830)
XLA Ops:
  7.8 0.7 and_select_fusion
  8.5 0.2 convert_reduce_fusion
  8.7 0.1 select_reduce_fusion.1
  8.8 0.8 all_to_all.11
  9.6 13.2 %all-to-all-start = ((s32[64,1,2]{2,1,0:T(1,128)}), s32[64,1,2]{2,1,0:T(1,128)S(1)}, u32[]{:S(2)}, u32[]{:S(2)}) async-start(s32[64,1,2]{2,1,0:T(1,128)} %bitcast.2), calls=%async_computation | async-start | bytes 65536 | tf_op jit(solution)/shard_map/all_to_all | solution.py:350
  22.7 1.1 copy.25
  23.8 8.1 %all-to-all-done = s32[64,1,2]{2,1,0:T(1,128)S(1)} async-done(((s32[64,1,2]{2,1,0:T(1,128)}), s32[64,1,2]{2,1,0:T(1,128)S(1)}, u32[]{:S(2)}, u32[]{:S(2)}) %all-to-all-start) | async-done | bytes 544 | tf_op jit(solution)/shard_map/all_to_all | solution.py:350
  31.9 0.1 copy.21
  32.0 0.1 copy.22
  32.1 0.1 reshape.72
  32.3 2.0 gather_fusion
  34.3 0.0 copy-start.3
  34.3 4.9 %all-to-all-start.1 = ((bf16[64,2,32,256]{3,2,1,0:T(8,128)(2,1)}), bf16[64,2,32,256]{3,2,1,0:T(8,128)(2,1)S(1)}, u32[]{:S(2)}, u32[]{:S(2)}) async-start(bf16[64,2,32,256]{3,2,1,0:T(8,128)(2,1)} %bitcast.4), calls=%async_computation.1 | async-start | bytes 4194304 | tf_op jit(solution)/shard_map/all_to_all | solution.py:352
  39.2 0.0 copy-start.1
  39.3 0.0 copy-start.2
  39.3 0.0 all-gather.3.cloned.1.call-start
  39.3 0.0 copy-done.3
  39.3 0.2 convert_reduce_fusion.1
  39.5 0.2 select_reduce_fusion
  39.7 50.9 %all-to-all-done.1 = bf16[64,2,32,256]{3,2,1,0:T(8,128)(2,1)S(1)} async-done(((bf16[64,2,32,256]{3,2,1,0:T(8,128)(2,1)}), bf16[64,2,32,256]{3,2,1,0:T(8,128)(2,1)S(1)}, u32[]{:S(2)}, u32[]{:S(2)}) %all-to-all-start.1) | async-done | bytes 2097184 | tf_op jit(solution)/shard_map/all_to_all | solution.py:352
  90.6 1.8 gather_fusion.1
  92.4 0.0 all-gather.3.cloned.1.call-update
  92.4 0.1 fusion.4
  92.6 0.1 slice_compare_fusion
  92.6 0.1 add_convert_fusion
  92.7 0.1 select_reduce_fusion.4.last_ref
  92.8 51.3 %all-gather.3.cloned.1.call-done.tiles_ref = bf16[72,128,256]{2,1,0:T(8,128)(2,1)} async-done(((bf16[72,32,256]{2,1,0:T(8,128)(2,1)}), bf16[72,128,256]{2,1,0:T(8,128)(2,1)}) %all-gather.3.cloned.1.call-update) | async-done | bytes 4718608 | tf_op jit(solution)/shard_map/all_gather | solution.py:355
  144.2 0.0 copy-done.1
  144.2 0.0 copy-done.2
  144.2 0.0 copy-start
  144.2 2.3 copy-done
  146.5 81.6 %shard_map.77 = (f32[32,2048]{1,0:T(8,128)S(1)}, f32[32,2048]{1,0:T(8,128)S(1)}) custom-call(s32[72]{0:T(128)S(1)} %get-tuple-element.4.perm_ref, s32[72]{0:T(128)S(1)} %get-tuple-element.3.user_ref, f32[72]{0:T(128)S(1)} %get-tuple-element.7.keep_ref, f32[72]{0:T(128)S(1)} %get-tuple-element.8.live_ref, s32[8]{0:T(128)S(1)} %select_reduce_fusion.4.last_ref, ...), custom_call_target="tpu_custom_call" | custom-call | tf_op jit(solution)/shard_map/pallas_call | solution.py:278
  228.1 0.7 copy.29
  228.8 0.7 copy.30
  (8 shorter events, 0.0 us)
Async XLA Ops:
  9.6 22.4 %all-to-all-start = ((s32[64,1,2]{2,1,0:T(1,128)}), s32[64,1,2]{2,1,0:T(1,128)S(1)}, u32[]{:S(2)}, u32[]{:S(2)}) async-start(s32[64,1,2]{2,1,0:T(1,128)} %bitcast.2), calls=%async_computation | async-start | bytes 65536 | tf_op jit(solution)/shard_map/all_to_all | solution.py:350
  34.3 5.0 %copy-start.3 = (s32[72]{0:T(128)S(1)}, s32[72]{0:T(128)}, u32[]{:S(2)}) copy-start(s32[72]{0:T(128)} %param.8) | copy-start | bytes 868
  34.3 56.3 %all-to-all-start.1 = ((bf16[64,2,32,256]{3,2,1,0:T(8,128)(2,1)}), bf16[64,2,32,256]{3,2,1,0:T(8,128)(2,1)S(1)}, u32[]{:S(2)}, u32[]{:S(2)}) async-start(bf16[64,2,32,256]{3,2,1,0:T(8,128)(2,1)} %bitcast.4), calls=%async_computation.1 | async-start | bytes 4194304 | tf_op jit(solution)/shard_map/all_to_all | solution.py:352
  39.2 104.9 %copy-start.1 = (bf16[32,8192]{1,0:T(8,128)(2,1)S(1)}, bf16[32,8192]{1,0:T(8,128)(2,1)}, u32[]{:S(2)}) copy-start(bf16[32,8192]{1,0:T(8,128)(2,1)} %items_ref.1) | copy-start | bytes 1572868
  39.3 104.9 %copy-start.2 = (f32[32,2048]{1,0:T(8,128)S(1)}, f32[32,2048]{1,0:T(8,128)}, u32[]{:S(2)}) copy-start(f32[32,2048]{1,0:T(8,128)} %users_ref.1) | copy-start | bytes 786436
  39.3 104.9 %all-gather.3.cloned.1.call-start = ((), (), s32[]{:S(2)}) async-start(), calls=%async_computation.2 | async-start | bytes 5898240 | tf_op jit(solution)/shard_map/all_gather | solution.py:355
  144.2 2.3 copy-start
Sparse Core Ops, SparseCore 0:
  92.6 51.5 all-gather.2

commit v2 on v1

v2 whole, which is shorter than its diff:
```python
import jax
import jax.numpy as jnp
from jax import lax
from jax.experimental import pallas as pl
from jax.experimental.pallas import tpu as pltpu
from jax.sharding import PartitionSpec as P

RIDGE = 0.5
CONFIDENCE = 40.0
HIGHEST = lax.Precision.HIGHEST
MESH = pl.DeviceIdType.MESH
F32 = jnp.float32
BF16 = jnp.bfloat16
Y_CHIPS = 4
Z_CHIPS = 8
CORES = 2
GROUP = 16
PLANE = Y_CHIPS * CORES
CAPACITY = 2
SLOTS = Z_CHIPS * CAPACITY
PIECES = 4
UNROLL = 24
VMEM_BYTES = 48 * 1024 * 1024


def interleave(first, second, odd):
    low = lax.broadcasted_iota(jnp.int32, first.shape, 1) < 64
    if odd:
        return jnp.where(low, pltpu.roll(first, 64, 1), second)
    return jnp.where(low, first, pltpu.roll(second, 64, 1))


def kernel(
    raw_ref, perm_ref, user_ref, keep_ref, live_ref, last_ref, has_ref,
    ask_ref, users_ref, items_ref, mask_ref,
    solution_ref, residual_ref,
    asked, asked_rows, asked_smem, ring_0, ring_1, ring_2, ring_3, plane_send,
    plane_recv_0, plane_recv_1, plane_recv_2, plane_recv_3, tiles, masks,
    users_send, users_recv, items_recv, gram_part, gram_recv, gram_piece, gram_all, gram,
    sums_send, sums_recv, halves, terms, state_x, state_r, state_d, image, out_send, out_recv,
    mask_sem, smem_sem, a_send, a_recv, z_send, z_recv, y_send, y_recv, x_send, x_recv,
    u_send, u_recv, i_send, i_recv, g_send, g_recv, s_send, s_recv, o_send, o_recv,
):
    rings = (ring_0, ring_1, ring_2, ring_3)
    plane_recvs = (plane_recv_0, plane_recv_1, plane_recv_2, plane_recv_3)
    row = lax.axis_index("rows")
    col = lax.axis_index("cols")
    n_cols = lax.axis_size("cols")
    core = lax.rem(row, CORES)
    own_z = lax.rem(lax.div(row, CORES), Z_CHIPS)
    own_y = lax.div(row, GROUP)
    own_a = lax.rem(row, GROUP)
    own_b = col * Y_CHIPS + own_y
    own_p = own_y * CORES + core
    tile_total, own_users, _ = masks.shape
    col_width = users_ref.shape[0]
    blocks = halves.shape[0]
    item_blocks = ring_0.shape[1]
    item_quarter = items_recv.shape[1]
    part = item_blocks // 2

    def peer_a(j):
        return (own_y * GROUP + j, col)

    def peer_b(j):
        return (lax.rem(j, Y_CHIPS) * GROUP + own_a, lax.div(j, Y_CHIPS))

    def peer_p(j):
        return (lax.div(j, CORES) * GROUP + own_z * CORES + lax.rem(j, CORES), col)

    def peer_c(j):
        return (row, j)

    z_peers = [
        (own_y * GROUP + lax.rem(own_z + step, Z_CHIPS) * CORES + core, col) for step in (1, Z_CHIPS - 1)
    ]
    right, left = lax.rem(col + 1, n_cols), lax.rem(col + n_cols - 1, n_cols)
    across = lax.rem(col + 2, n_cols)

    def others(own, count, body):
        def step(i, carry):
            body(lax.rem(own + i, count))
            return carry

        lax.fori_loop(1, count, step, 0)

    def remote(src, dst, send_sem, recv_sem, peer):
        return pltpu.make_async_remote_copy(
            src_ref=src, dst_ref=dst, send_sem=send_sem, recv_sem=recv_sem, device_id=peer, device_id_type=MESH
        )

    mask_copy = pltpu.make_async_copy(
        mask_ref.at[:, pl.ds(pl.multiple_of(col * own_users, own_users), own_users), :], masks, mask_sem
    )
    mask_copy.start()

    barrier = pltpu.get_barrier_semaphore()

    def greet(peer):
        pl.semaphore_signal(barrier, inc=1, device_id=peer, device_id_type=MESH)

    others(own_a, GROUP, lambda j: greet(peer_a(j)))
    others(own_b, GROUP, lambda j: greet(peer_b(j)))
    others(own_y, Y_CHIPS, lambda j: greet(peer_p(j * CORES + 1 - core)))

    def split_items(b, carry):
        block = items_ref[:, pl.ds(pl.multiple_of(b * 256, 256), 256)]
        for piece in range(PIECES):
            lane, sub = piece // 2, piece % 2
            rings[piece][0, b] = block[16 * sub : 16 * sub + 16, 128 * lane : 128 * lane + 128]
        return carry

    lax.fori_loop(0, item_blocks, split_items, 0, unroll=4)
    for dest in range(n_cols):
        for pair in range(blocks // 2):
            at = (dest // 2) * 128
            first = users_ref[:, pl.ds(2 * pair * 256 + at, 128)]
            second = users_ref[:, pl.ds((2 * pair + 1) * 256 + at, 128)]
            users_send[dest, :, pl.ds(pair * 128, 128)] = interleave(first, second, dest % 2 == 1)
    pl.semaphore_wait(barrier, 2 * (GROUP - 1) + Y_CHIPS - 1)

    def z_copy(piece, way, step, h):
        if way == 0:
            src, dst = (Z_CHIPS - step) % Z_CHIPS, Z_CHIPS - 1 - step
        else:
            src, dst = step, step + 1
        chunk = pl.ds(part * h, part)
        return remote(
            rings[piece].at[src, chunk], rings[piece].at[dst, chunk],
            z_send.at[piece, way, step, h], z_recv.at[piece, way, step, h], z_peers[way],
        )

    last_step = Z_CHIPS // 2 - 1

    def z_travels(step, way, h):
        return step < last_step or h == way

    def z_begin(piece):
        for h in range(2):
            for way in range(2):
                z_copy(piece, way, 0, h).start()

    def z_step(piece, step):
        for h in range(2):
            for way in range(2):
                z_copy(piece, way, step - 1, h).wait_recv()
                if z_travels(step, way, h):
                    z_copy(piece, way, step, h).start()

    def z_end(piece):
        for way in range(2):
            z_copy(piece, way, last_step, way).wait_recv()

    def ask_copy(j, slot):
        return remote(ask_ref.at[j], asked.at[slot], a_send.at[j], a_recv.at[slot], peer_p(j))

    def plane_copy(piece, j, slot):
        return remote(
            plane_send.at[piece, j], plane_recvs[piece].at[pl.ds(pl.multiple_of(slot * SLOTS, SLOTS), SLOTS)],
            y_send.at[piece, j], y_recv.at[piece, slot], peer_p(j),
        )

    def plane_begin(piece):
        def pick(j, carry):
            for slot in range(SLOTS):
                plane_send[piece, j, slot] = rings[piece][slot // CAPACITY, asked_smem[j, slot]]
            return carry

        lax.fori_loop(0, PLANE, pick, 0)
        others(own_p, PLANE, lambda j: plane_copy(piece, j, own_p).start())
        plane_recvs[piece][pl.ds(pl.multiple_of(own_p * SLOTS, SLOTS), SLOTS)] = plane_send[piece, own_p]

    def x_ref(piece, owner):
        rows_at = pl.multiple_of(owner * col_width + 16 * (piece % 2), 16)
        return tiles.at[piece // 2, :, pl.ds(rows_at, 16), :]

    def x_copy(piece, kind, owner, peer):
        return remote(
            x_ref(piece, owner), x_ref(piece, owner), x_send.at[piece, kind], x_recv.at[piece, kind], (row, peer)
        )

    def x_begin(piece):
        others(own_p, PLANE, lambda j: plane_copy(piece, j, j).wait_recv())
        rows_at = pl.multiple_of(col * col_width + 16 * (piece % 2), 16)

        def pack(s, carry):
            tiles[piece // 2, s, pl.ds(rows_at, 16), :] = plane_recvs[piece][raw_ref[s]]
            return carry

        lax.fori_loop(0, tile_total, pack, 0, unroll=8)
        x_copy(piece, 0, col, right).start()
        x_copy(piece, 1, col, left).start()

    def x_forward(piece):
        if piece % 2 == 0:
            x_copy(piece, 0, left, right).wait_recv()
            x_copy(piece, 2, left, right).start()
        else:
            x_copy(piece, 1, right, left).wait_recv()
            x_copy(piece, 2, right, left).start()

    def x_end(piece):
        if piece % 2 == 0:
            x_copy(piece, 1, right, left).wait_recv()
        else:
            x_copy(piece, 0, left, right).wait_recv()
        x_copy(piece, 2, across, left).wait_recv()

    own_cols = pl.ds(pl.multiple_of(col * col_width, col_width), col_width)

    def item_quarter_ref(j):
        return items_ref.at[:, pl.ds(pl.multiple_of(j * item_quarter, item_quarter), item_quarter)]

    def col_rows(j):
        return pl.ds(pl.multiple_of(j * col_width, col_width), col_width)

    def item_copy(j, slot):
        return remote(item_quarter_ref(j), items_recv.at[col_rows(slot)], i_send.at[j], i_recv.at[slot], peer_c(j))

    def user_copy(j, slot):
        return remote(users_send.at[j], users_recv.at[col_rows(slot)], u_send.at[j], u_recv.at[slot], peer_c(j))

    def gram_first(j, slot):
        return remote(gram_part.at[j], gram_recv.at[slot], g_send.at[0, j], g_recv.at[0, slot], peer_a(j))

    def gram_second(j, slot):
        return remote(gram_piece, gram_all.at[slot], g_send.at[1, j], g_recv.at[1, slot], peer_b(j))

    def gram_third(j, slot):
        return remote(gram.at[own_a], gram.at[slot], g_send.at[2, j], g_recv.at[2, slot], peer_a(j))

    def gram_1():
        others(col, n_cols, lambda j: item_copy(j, j).wait_recv())
        table = items_recv[...]
        gram_part[...] = lax.dot_general(
            table, table, (((1,), (1,)), ((), ())), preferred_element_type=F32
        ).reshape(gram_part.shape)
        others(own_a, GROUP, lambda j: gram_first(j, own_a).start())
        gram_recv[own_a] = gram_part[own_a]

    def gram_2():
        others(own_a, GROUP, lambda j: gram_first(j, j).wait_recv())
        gram_piece[...] = jnp.sum(gram_recv[...], axis=0)
        others(own_b, GROUP, lambda j: gram_second(j, own_b).start())
        gram_all[own_b] = gram_piece[...]

    def gram_3():
        others(own_b, GROUP, lambda j: gram_second(j, j).wait_recv())
        gram[own_a] = jnp.sum(gram_all[...], axis=0)
        others(own_a, GROUP, lambda j: gram_third(j, own_a).start())

    def sparse_part(vectors, lanes, first_time):
        high = vectors.astype(BF16)
        low = (vectors - high.astype(F32)).astype(BF16)
        halves[:, :own_users] = high.reshape(blocks, own_users, 128)
        halves[:, own_users:] = low.reshape(blocks, own_users, 128)

        def step(s, running):
            if len(lanes) == 2:
                item = jnp.concatenate([tiles[0, s], tiles[1, s]], axis=1)
                mask = masks[perm_ref[s]]
            else:
                item = tiles[lanes[0], s]
                mask = masks[perm_ref[s], :, pl.ds(128 * lanes[0], 128)]
            mask = mask.astype(F32) * live_ref[s]
            scores = jnp.dot(halves[user_ref[s]], item, preferred_element_type=F32)
            scores = scores[:own_users] + scores[own_users:]
            if first_time:
                strengths = mask * ((1.0 + CONFIDENCE) - CONFIDENCE * scores)
            else:
                strengths = mask * scores
            s_high = strengths.astype(BF16)
            s_low = (strengths - s_high.astype(F32)).astype(BF16)
            both = lax.dot_general(
                jnp.concatenate([s_high, s_low], axis=0), item, (((1,), (1,)), ((), ())),
                preferred_element_type=F32,
            )
            running = both[:own_users] + both[own_users:] + keep_ref[s] * running
            terms[s] = running
            return running

        lax.fori_loop(0, tile_total, step, jnp.zeros((own_users, 128), F32), unroll=UNROLL)
        return jnp.concatenate([terms[last_ref[b]] * has_ref[b] for b in range(blocks)], axis=0)

    def dense_part(vectors):
        return (
            jnp.dot(vectors, gram[...].reshape(128, 128), precision=HIGHEST, preferred_element_type=F32)
            + RIDGE * vectors
        )

    def sums_copy(at, peer, j, slot):
        return remote(sums_send.at[at], sums_recv.at[at, slot], s_send.at[at, j], s_recv.at[at, slot], peer(j))

    def all_sums(index, products):
        rows = [jnp.sum(p, axis=0, keepdims=True) for p in products]
        rows.append(jnp.zeros((8 - len(rows), 128), F32))
        total = jnp.concatenate(rows, axis=0)
        for stage, (peer, own) in enumerate(((peer_a, own_a), (peer_b, own_b))):
            at = 2 * index + stage
            sums_send[at] = total
            others(own, GROUP, lambda j: sums_copy(at, peer, j, own).start())
            sums_recv[at, own] = total
            others(own, GROUP, lambda j: sums_copy(at, peer, j, j).wait_recv())
            total = jnp.sum(sums_recv[at], axis=0)
        total = jnp.sum(total, axis=1, keepdims=True)
        return [total[i : i + 1, :] for i in range(len(products))]

    def out_copy(index, j, slot):
        return remote(
            out_send.at[index, j], out_recv.at[index, slot], o_send.at[index, j], o_recv.at[index, slot], peer_c(j)
        )

    def out_begin(index, vectors):
        out_send[index] = vectors.T.reshape(n_cols, col_width, blocks * own_users)
        others(col, n_cols, lambda j: out_copy(index, j, col).start())
        out_recv[index, col] = out_send[index, col]

    def out_end(index):
        others(col, n_cols, lambda j: out_copy(index, j, j).wait_recv())

    z_begin(0)
    others(own_p, PLANE, lambda j: ask_copy(j, own_p).start())
    asked[own_p] = ask_ref[own_p]
    others(col, n_cols, lambda j: item_copy(j, col).start())
    others(col, n_cols, lambda j: user_copy(j, col).start())
    items_recv[own_cols, :] = item_quarter_ref(col)[...]
    users_recv[own_cols, :] = users_send[col]

    others(own_p, PLANE, lambda j: ask_copy(j, j).wait_recv())
    asked_rows[...] = asked[:, 0, :]
    to_smem = pltpu.make_async_copy(asked_rows, asked_smem, smem_sem)
    to_smem.start()
    to_smem.wait()

    for piece in range(PIECES):
        z_step(piece, 1)
        if piece == 1:
            gram_2()
        if piece >= 2:
            x_forward(piece - 2)
        z_step(piece, 2)
        if piece == 0:
            gram_1()
        if piece >= 1:
            x_begin(piece - 1)
        z_step(piece, 3)
        if piece + 1 < PIECES:
            z_begin(piece + 1)
        z_end(piece)
        plane_begin(piece)
        if piece == 1:
            gram_3()
    x_forward(PIECES - 2)
    x_begin(PIECES - 1)
    others(col, n_cols, lambda j: user_copy(j, j).wait_recv())
    state_x[...] = users_recv[...].T
    mask_copy.wait()
    others(own_a, GROUP, lambda j: gram_third(j, j).wait_recv())
    x_end(0)
    x_end(1)
    state_r[...] = sparse_part(state_x[...], (0,), True) - dense_part(state_x[...])
    x_forward(PIECES - 1)
    x_end(2)
    x_end(3)

    state_r[...] += sparse_part(state_x[...], (1,), True)
    out_begin(0, state_r[...])
    image[...] = dense_part(state_r[...]) + CONFIDENCE * sparse_part(state_r[...], (0, 1), False)
    out_begin(1, image[...])
    norm_0, curve_0 = all_sums(0, [state_r[...] * state_r[...], state_r[...] * image[...]])
    alpha_0 = norm_0 / curve_0
    state_d[...] = state_r[...]
    state_r[...] = state_r[...] - alpha_0 * image[...]

    image_r = dense_part(state_r[...]) + CONFIDENCE * sparse_part(state_r[...], (0, 1), False)
    out_begin(2, image_r)
    norm_1, curve_rr, curve_rd, curve_dr = all_sums(
        1,
        [
            state_r[...] * state_r[...],
            state_r[...] * image_r,
            state_r[...] * image[...],
            state_d[...] * image_r,
        ],
    )
    beta = norm_1 / norm_0
    alpha_1 = norm_1 / (curve_rr + beta * (curve_rd + curve_dr) + beta * beta * curve_0)

    for index in range(3):
        out_end(index)
    for block in range(blocks):
        lanes = pl.ds((block // 2) * 128, 128)
        for side in range(n_cols // 2):
            start_r, image_d, image_1 = [
                interleave(out_recv[i, 2 * side, :, lanes], out_recv[i, 2 * side + 1, :, lanes], block % 2 == 1)
                for i in range(3)
            ]
            here = pl.ds(block * 256 + side * 128, 128)
            mid_r = start_r - alpha_0 * image_d
            mid_x = users_ref[:, here] + alpha_0 * start_r
            solution_ref[:, here] = mid_x + alpha_1 * (mid_r + beta * start_r)
            residual_ref[:, here] = mid_r - alpha_1 * (image_1 + beta * image_d)

    others(own_p, PLANE, lambda j: ask_copy(j, own_p).wait_send())
    others(col, n_cols, lambda j: item_copy(j, col).wait_send())
    others(col, n_cols, lambda j: user_copy(j, col).wait_send())
    others(own_a, GROUP, lambda j: gram_first(j, own_a).wait_send())
    others(own_b, GROUP, lambda j: gram_second(j, own_b).wait_send())
    others(own_a, GROUP, lambda j: gram_third(j, own_a).wait_send())
    for piece in range(PIECES):
        for step in range(last_step + 1):
            for way in range(2):
                for h in range(2):
                    if z_travels(step, way, h):
                        z_copy(piece, way, step, h).wait_send()
        others(own_p, PLANE, lambda j: plane_copy(piece, j, own_p).wait_send())
        x_copy(piece, 0, col, right).wait_send()
        x_copy(piece, 1, col, left).wait_send()
        x_copy(piece, 2, left, right).wait_send()
    for index in range(2):
        others(own_a, GROUP, lambda j: sums_copy(2 * index, peer_a, j, own_a).wait_send())
        others(own_b, GROUP, lambda j: sums_copy(2 * index + 1, peer_b, j, own_b).wait_send())
    for index in range(3):
        others(col, n_cols, lambda j: out_copy(index, j, col).wait_send())


def solve(tables, ask, user_factors, item_factors, tile_mask, n_cols):
    col_width, users = user_factors.shape
    slots, tile_rows, tile_cols = tile_mask.shape
    width = col_width * n_cols
    blocks = users // tile_rows
    item_blocks = item_factors.shape[1] // tile_rows
    own_users = tile_rows // n_cols
    mine = blocks * own_users
    item_quarter = item_factors.shape[1] // n_cols
    vmem = pl.BlockSpec(memory_space=pltpu.VMEM)
    smem = pl.BlockSpec(memory_space=pltpu.SMEM)
    piece = width // GROUP
    out = jax.ShapeDtypeStruct((col_width, users), F32)
    dma = pltpu.SemaphoreType.DMA
    return pl.pallas_call(
        kernel,
        out_shape=(out, out),
        in_specs=[smem] * 7 + [vmem] * 3 + [pl.BlockSpec(memory_space=pl.ANY)],
        out_specs=(vmem, vmem),
        scratch_shapes=[
            pltpu.VMEM((PLANE, 8, 128), jnp.int32),
            pltpu.VMEM((PLANE, 128), jnp.int32),
            pltpu.SMEM((PLANE, 128), jnp.int32),
            *[pltpu.VMEM((Z_CHIPS, item_blocks, 16, 128), BF16)] * PIECES,
            pltpu.VMEM((PIECES, PLANE, SLOTS, 16, 128), BF16),
            *[pltpu.VMEM((PLANE * SLOTS, 16, 128), BF16)] * PIECES,
            pltpu.VMEM((2, slots, width, 128), BF16),
            pltpu.VMEM((slots, own_users, tile_cols), BF16),
            pltpu.VMEM((n_cols, col_width, mine), F32),
            pltpu.VMEM((width, mine), F32),
            pltpu.VMEM((width, item_quarter), BF16),
            pltpu.VMEM((GROUP, piece, width), F32),
            pltpu.VMEM((GROUP, piece, width), F32),
            pltpu.VMEM((piece, width), F32),
            pltpu.VMEM((GROUP, piece, width), F32),
            pltpu.VMEM((GROUP, piece, width), F32),
            pltpu.VMEM((4, 8, 128), F32),
            pltpu.VMEM((4, GROUP, 8, 128), F32),
            pltpu.VMEM((blocks, 2 * own_users, width), BF16),
            pltpu.VMEM((slots, own_users, width), F32),
            pltpu.VMEM((mine, width), F32),
            pltpu.VMEM((mine, width), F32),
            pltpu.VMEM((mine, width), F32),
            pltpu.VMEM((mine, width), F32),
            pltpu.VMEM((3, n_cols, col_width, mine), F32),
            pltpu.VMEM((3, n_cols, col_width, mine), F32),
            dma,
            dma,
            dma((PLANE,)),
            dma((PLANE,)),
            dma((PIECES, 2, Z_CHIPS // 2, 2)),
            dma((PIECES, 2, Z_CHIPS // 2, 2)),
            dma((PIECES, PLANE)),
            dma((PIECES, PLANE)),
            dma((PIECES, 3)),
            dma((PIECES, 3)),
            dma((n_cols,)),
            dma((n_cols,)),
            dma((n_cols,)),
            dma((n_cols,)),
            dma((3, GROUP)),
            dma((3, GROUP)),
            dma((4, GROUP)),
            dma((4, GROUP)),
            dma((3, n_cols)),
            dma((3, n_cols)),
        ],
        compiler_params=pltpu.CompilerParams(
            collective_id=0, has_side_effects=True, vmem_limit_bytes=VMEM_BYTES
        ),
    )(*tables, ask, user_factors, item_factors, tile_mask)


def on_device(user_factors, item_factors, tile_user, tile_item, tile_count, tile_mask):
    n_cols = lax.axis_size("cols")
    tile_rows = tile_mask.shape[1]
    slots = tile_user.shape[0]
    blocks = user_factors.shape[1] // tile_rows
    item_blocks = item_factors.shape[1] // tile_rows
    own_z = lax.axis_index("rows") // CORES % Z_CHIPS

    order = jnp.arange(slots, dtype=jnp.int32)
    live = order < tile_count[0]
    key = jnp.where(live, tile_user, blocks) * slots + order
    place = jnp.sum((key[None, :] < key[:, None]).astype(jnp.int32), axis=1)
    chosen = (place[None, :] == order[:, None]).astype(jnp.int32)
    perm = jnp.sum(chosen * order[None, :], axis=1)
    user = jnp.sum(chosen * tile_user[None, :], axis=1)
    live_sorted = live.astype(F32)
    keep = jnp.concatenate([jnp.zeros((1,), F32), (user[1:] == user[:-1]).astype(F32)])
    per_block = (user[None, :] == jnp.arange(blocks, dtype=jnp.int32)[:, None]) & live[None, :]
    has = jnp.any(per_block, axis=1).astype(F32)
    last = jnp.max(jnp.where(per_block, order[None, :], 0), axis=1)

    holder = tile_item // item_blocks
    earlier = (holder[None, :] == holder[:, None]) & (order[None, :] < order[:, None]) & live[None, :]
    rank = jnp.minimum(jnp.sum(earlier.astype(jnp.int32), axis=1), CAPACITY - 1)
    peer = holder // GROUP * CORES + holder % CORES
    distance = (holder // CORES % Z_CHIPS - own_z + Z_CHIPS) % Z_CHIPS
    raw = jnp.where(live, peer * SLOTS + distance * CAPACITY + rank, 0)
    raw_range = jnp.arange(PLANE * SLOTS, dtype=jnp.int32)
    hits = ((raw[None, :] == raw_range[:, None]) & live[None, :]).astype(jnp.int32)
    ask = jnp.sum(hits * (tile_item % item_blocks)[None, :], axis=1).reshape(PLANE, 1, SLOTS)
    ask = jnp.pad(ask, ((0, 0), (0, 7), (0, 128 - SLOTS)))
    raw_sorted = jnp.sum(chosen * raw[None, :], axis=1)
    return solve(
        (raw_sorted, perm, user, keep, live_sorted, last, has), ask, user_factors, item_factors, tile_mask, n_cols
    )


def solution(mesh):
    return jax.shard_map(
        on_device,
        mesh=mesh,
        in_specs=(
            P("cols", "rows"),
            P("cols", "rows"),
            P("rows"),
            P("rows"),
            P("rows"),
            P("rows", None, None),
        ),
        out_specs=(P("cols", "rows"), P("cols", "rows")),
        check_vma=False,
    )
```

time: 237 us -> 144 us (0.61)
  waiting for transfers between devices: 110 us -> 0 us
  Pallas kernels: 81.6 us -> 136 us
  starting transfers between devices: 18.1 us -> 0 us
  between operations: 14.8 us -> 1.36 us
  local copies, waits for them, and re-layouts: 9.78 us -> 3.48 us
    all_to_all x2 -> x0, waiting for transfers between devices: 59 us -> none  [the longest x1 50.9 us: on_device(): lax.all_to_all(shards[wanted], 'rows', split_axis=0, concat_axis=0, tiled...]
    pallas_call x1, Pallas kernels: 81.6 us -> 136 us  [solve(): pl.pallas_call(kernel, out_shape=(out, out), in_specs=[smem] * 7 + [vmem]...]
    all_gather x1 -> x0, waiting for transfers between devices: 51.3 us -> none  [on_device(): tiles = lax.all_gather(picked, 'cols', axis=1, tiled=True)]
    all_to_all x2 -> x0, starting transfers between devices: 18.1 us -> none  [the longest x1 13.2 us: on_device(): lax.all_to_all(requests, 'rows', split_axis=0, concat_axis=0, tiled=True)]
    gather x2 -> x0, local copies, waits for them, and re-layouts: 3.84 us -> none  [the longest x1 2.03 us: on_device(): shards[wanted]]
  transfers between devices with their start and end apart: 3 -> 0, of which waited for: 3 -> 0; matrix products, arithmetic and copies ran while one was open for 1% -> 0% of each run, Pallas kernels for 0% -> 0%
where the time goes in v2:
time: 144 us
  Pallas kernels  136 us (94%)
  local copies, waits for them, and re-layouts  3.48 us (2%)
  other arithmetic  3.05 us (2%)
    pallas_call x1, Pallas kernels, solve(): pl.pallas_call(kernel, out_shape=(out, out), in_specs=[smem] * 7 + [vmem]...  136 us
    unnamed x6, local copies, waits for them, and re-layouts  3.39 us

profile of v2, /device:TPU:1, one launch (start us, length us, event | category | flops | bytes accessed | tf_op | source)
XLA Modules:
  0.0 143.6 jit_solution(8433629425629759069)
XLA Ops:
  1.3 0.7 and_select_fusion
  2.0 0.2 convert_reduce_fusion
  2.2 0.7 iota_add_fusion
  2.9 0.2 convert_reduce_fusion.1
  3.0 0.1 select_reduce_fusion
  3.2 0.8 select_reduce_fusion.1
  4.0 0.1 select_reduce_fusion.4.last_ref
  4.1 0.1 fusion.4
  4.2 0.1 slice_compare_fusion
  4.3 0.1 add_convert_fusion.keep_ref
  4.4 0.1 reshape.20
  4.5 0.0 copy-start
  4.5 1.0 copy-done
  5.5 0.0 copy-start.1
  5.5 0.9 copy-done.1
  6.5 135.7 %shard_map.77 = (f32[32,2048]{1,0:T(8,128)S(1)}, f32[32,2048]{1,0:T(8,128)S(1)}) custom-call(s32[72]{0:T(128)S(1)} %get-tuple-element.4.raw_ref, s32[72]{0:T(128)S(1)} %get-tuple-element.3.perm_ref, s32[72]{0:T(128)S(1)} %get-tuple-element.2.user_ref, f32[72]{0:T(128)S(1)} %add_convert_fusion.keep_ref, f32[72]{0:T(128)S(1)} %fusion.14.live_ref, ...), custom_call_target="tpu_custom_call" | custom-call | tf_op jit(solution)/shard_map/pallas_call | solution.py:441
  142.2 0.7 copy.13
  142.9 0.7 copy.14
  (4 shorter events, 0.0 us)
Async XLA Ops:
  4.5 1.0 copy-start
  5.5 0.9 copy-start.1

commit v3 on v2

--- a/solution.py
+++ b/solution.py
@@ -19,6 +19,8 @@
 CAPACITY = 2
 SLOTS = Z_CHIPS * CAPACITY
 PIECES = 4
+CHUNKS = 4
+NEAR = SLOTS - CAPACITY
 UNROLL = 24
 VMEM_BYTES = 48 * 1024 * 1024
 
@@ -31,10 +33,10 @@
 
 
 def kernel(
-    raw_ref, perm_ref, user_ref, keep_ref, live_ref, last_ref, has_ref,
+    holder_ref, place_ref, perm_ref, user_ref, keep_ref, live_ref, last_ref, has_ref,
     ask_ref, users_ref, items_ref, mask_ref,
     solution_ref, residual_ref,
-    asked, asked_rows, asked_smem, ring_0, ring_1, ring_2, ring_3, plane_send,
+    asked, asked_rows, asked_smem, ring_0, ring_1, ring_2, ring_3, far_0, far_1, far_2, far_3, plane_send,
     plane_recv_0, plane_recv_1, plane_recv_2, plane_recv_3, tiles, masks,
     users_send, users_recv, items_recv, gram_part, gram_recv, gram_piece, gram_all, gram,
     sums_send, sums_recv, halves, terms, state_x, state_r, state_d, image, out_send, out_recv,
@@ -42,6 +44,7 @@
     u_send, u_recv, i_send, i_recv, g_send, g_recv, s_send, s_recv, o_send, o_recv,
 ):
     rings = (ring_0, ring_1, ring_2, ring_3)
+    fars = (far_0, far_1, far_2, far_3)
     plane_recvs = (plane_recv_0, plane_recv_1, plane_recv_2, plane_recv_3)
     row = lax.axis_index("rows")
     col = lax.axis_index("cols")
@@ -57,7 +60,7 @@
     blocks = halves.shape[0]
     item_blocks = ring_0.shape[1]
     item_quarter = items_recv.shape[1]
-    part = item_blocks // 2
+    part = item_blocks // CHUNKS
 
     def peer_a(j):
         return (own_y * GROUP + j, col)
@@ -74,8 +77,6 @@
     z_peers = [
         (own_y * GROUP + lax.rem(own_z + step, Z_CHIPS) * CORES + core, col) for step in (1, Z_CHIPS - 1)
     ]
-    right, left = lax.rem(col + 1, n_cols), lax.rem(col + n_cols - 1, n_cols)
-    across = lax.rem(col + 2, n_cols)
 
     def others(own, count, body):
         def step(i, carry):
@@ -120,91 +121,80 @@
     pl.semaphore_wait(barrier, 2 * (GROUP - 1) + Y_CHIPS - 1)
 
     def z_copy(piece, way, step, h):
+        chunk = pl.ds(part * h, part)
         if way == 0:
-            src, dst = (Z_CHIPS - step) % Z_CHIPS, Z_CHIPS - 1 - step
+            src = (Z_CHIPS - 1 - step) % (Z_CHIPS - 1)
+            dst = Z_CHIPS - 2 - step
         else:
             src, dst = step, step + 1
-        chunk = pl.ds(part * h, part)
+        target = rings[piece].at[dst, chunk] if step < last_step else fars[piece].at[chunk]
         return remote(
-            rings[piece].at[src, chunk], rings[piece].at[dst, chunk],
+            rings[piece].at[src, chunk], target,
             z_send.at[piece, way, step, h], z_recv.at[piece, way, step, h], z_peers[way],
         )
 
     last_step = Z_CHIPS // 2 - 1
 
     def z_travels(step, way, h):
-        return step < last_step or h == way
-
-    def z_begin(piece):
-        for h in range(2):
+        return step < last_step or (h < CHUNKS // 2) == (way == 0)
+
+    def z_step(piece, step):
+        for h in range(CHUNKS):
             for way in range(2):
-                z_copy(piece, way, 0, h).start()
-
-    def z_step(piece, step):
-        for h in range(2):
-            for way in range(2):
-                z_copy(piece, way, step - 1, h).wait_recv()
-                if z_travels(step, way, h):
+                if step > 0 and z_travels(step - 1, way, h):
+                    z_copy(piece, way, step - 1, h).wait_recv()
+                if step <= last_step and z_travels(step, way, h):
                     z_copy(piece, way, step, h).start()
-
-    def z_end(piece):
-        for way in range(2):
-            z_copy(piece, way, last_step, way).wait_recv()
 
     def ask_copy(j, slot):
         return remote(ask_ref.at[j], asked.at[slot], a_send.at[j], a_recv.at[slot], peer_p(j))
 
-    def plane_copy(piece, j, slot):
+    def plane_copy(piece, half, j, slot):
+        first, count = ((0, NEAR), (NEAR, CAPACITY))[half]
         return remote(
-            plane_send.at[piece, j], plane_recvs[piece].at[pl.ds(pl.multiple_of(slot * SLOTS, SLOTS), SLOTS)],
-            y_send.at[piece, j], y_recv.at[piece, slot], peer_p(j),
+            plane_send.at[piece, j, pl.ds(first, count)], plane_recvs[piece].at[slot, pl.ds(first, count)],
+            y_send.at[piece, half, j], y_recv.at[piece, half, slot], peer_p(j),
         )
 
-    def plane_begin(piece):
+    def plane_begin(piece, half):
+        first, count = ((0, NEAR), (NEAR, CAPACITY))[half]
+
         def pick(j, carry):
-            for slot in range(SLOTS):
-                plane_send[piece, j, slot] = rings[piece][slot // CAPACITY, asked_smem[j, slot]]
+            for slot in range(first, first + count):
+                if half == 0:
+                    block = rings[piece][slot // CAPACITY, asked_smem[j, slot]]
+                else:
+                    block = fars[piece][asked_smem[j, slot]]
+                plane_send[piece, j, slot] = block
             return carry
 
-        lax.fori_loop(0, PLANE, pick, 0)
-        others(own_p, PLANE, lambda j: plane_copy(piece, j, own_p).start())
-        plane_recvs[piece][pl.ds(pl.multiple_of(own_p * SLOTS, SLOTS), SLOTS)] = plane_send[piece, own_p]
+        lax.fori_loop(0, PLANE, pick, 0, unroll=2)
+        others(own_p, PLANE, lambda j: plane_copy(piece, half, j, own_p).start())
+        plane_recvs[piece][own_p, pl.ds(first, count)] = plane_send[piece, own_p, pl.ds(first, count)]
 
     def x_ref(piece, owner):
         rows_at = pl.multiple_of(owner * col_width + 16 * (piece % 2), 16)
         return tiles.at[piece // 2, :, pl.ds(rows_at, 16), :]
 
-    def x_copy(piece, kind, owner, peer):
+    def x_copy(piece, j, slot):
         return remote(
-            x_ref(piece, owner), x_ref(piece, owner), x_send.at[piece, kind], x_recv.at[piece, kind], (row, peer)
+            x_ref(piece, slot), x_ref(piece, slot), x_send.at[piece, j], x_recv.at[piece, slot], peer_c(j)
         )
 
     def x_begin(piece):
-        others(own_p, PLANE, lambda j: plane_copy(piece, j, j).wait_recv())
+        for half in range(2):
+            others(own_p, PLANE, lambda j: plane_copy(piece, half, j, j).wait_recv())
         rows_at = pl.multiple_of(col * col_width + 16 * (piece % 2), 16)
 
         def pack(s, carry):
-            tiles[piece // 2, s, pl.ds(rows_at, 16), :] = plane_recvs[piece][raw_ref[s]]
+            tiles[piece // 2, s, pl.ds(rows_at, 16), :] = plane_recvs[piece][holder_ref[s], place_ref[s]]
             return carry
 
         lax.fori_loop(0, tile_total, pack, 0, unroll=8)
-        x_copy(piece, 0, col, right).start()
-        x_copy(piece, 1, col, left).start()
-
-    def x_forward(piece):
-        if piece % 2 == 0:
-            x_copy(piece, 0, left, right).wait_recv()
-            x_copy(piece, 2, left, right).start()
-        else:
-            x_copy(piece, 1, right, left).wait_recv()
-            x_copy(piece, 2, right, left).start()
+        others(col, n_cols, lambda j: x_copy(piece, j, col).start())
 
     def x_end(piece):
-        if piece % 2 == 0:
-            x_copy(piece, 1, right, left).wait_recv()
-        else:
-            x_copy(piece, 0, left, right).wait_recv()
-        x_copy(piece, 2, across, left).wait_recv()
+        others(col, n_cols, lambda j: x_copy(piece, j, j).wait_recv())
 
     own_cols = pl.ds(pl.multiple_of(col * col_width, col_width), col_width)
 
@@ -291,19 +281,19 @@
     def sums_copy(at, peer, j, slot):
         return remote(sums_send.at[at], sums_recv.at[at, slot], s_send.at[at, j], s_recv.at[at, slot], peer(j))
 
-    def all_sums(index, products):
+    def all_sums(products):
         rows = [jnp.sum(p, axis=0, keepdims=True) for p in products]
         rows.append(jnp.zeros((8 - len(rows), 128), F32))
-        total = jnp.concatenate(rows, axis=0)
-        for stage, (peer, own) in enumerate(((peer_a, own_a), (peer_b, own_b))):
-            at = 2 * index + stage
+        total = jnp.sum(jnp.concatenate(rows, axis=0), axis=1, keepdims=True)
+        at_lane = lax.broadcasted_iota(jnp.int32, (8, 128), 0) == lax.broadcasted_iota(jnp.int32, (8, 128), 1)
+        total = jnp.sum(jnp.where(at_lane, total, 0.0), axis=0, keepdims=True)
+        for at, (peer, own) in enumerate(((peer_a, own_a), (peer_b, own_b))):
             sums_send[at] = total
             others(own, GROUP, lambda j: sums_copy(at, peer, j, own).start())
             sums_recv[at, own] = total
             others(own, GROUP, lambda j: sums_copy(at, peer, j, j).wait_recv())
             total = jnp.sum(sums_recv[at], axis=0)
-        total = jnp.sum(total, axis=1, keepdims=True)
-        return [total[i : i + 1, :] for i in range(len(products))]
+        return [total[:, i : i + 1] for i in range(len(products))]
 
     def out_copy(index, j, slot):
         return remote(
@@ -318,7 +308,7 @@
     def out_end(index):
         others(col, n_cols, lambda j: out_copy(index, j, j).wait_recv())
 
-    z_begin(0)
+    z_step(0, 0)
     others(own_p, PLANE, lambda j: ask_copy(j, own_p).start())
     asked[own_p] = ask_ref[own_p]
     others(col, n_cols, lambda j: item_copy(j, col).start())
@@ -332,34 +322,32 @@
     to_smem.start()
     to_smem.wait()
 
-    for piece in range(PIECES):
-        z_step(piece, 1)
-        if piece == 1:
+    span = last_step + 2
+    for time in range(1, 2 * (PIECES - 1) + span):
+        for piece in range(PIECES):
+            step = time - 2 * piece
+            if 0 <= step < span:
+                z_step(piece, step)
+                if step == span - 2:
+                    plane_begin(piece, 0)
+                if step == span - 1:
+                    plane_begin(piece, 1)
+            if step == span:
+                x_begin(piece)
+        if time == 2:
+            gram_1()
+        if time == 4:
             gram_2()
-        if piece >= 2:
-            x_forward(piece - 2)
-        z_step(piece, 2)
-        if piece == 0:
-            gram_1()
-        if piece >= 1:
-            x_begin(piece - 1)
-        z_step(piece, 3)
-        if piece + 1 < PIECES:
-            z_begin(piece + 1)
-        z_end(piece)
-        plane_begin(piece)
-        if piece == 1:
+        if time == 5:
             gram_3()
-    x_forward(PIECES - 2)
-    x_begin(PIECES - 1)
     others(col, n_cols, lambda j: user_copy(j, j).wait_recv())
     state_x[...] = users_recv[...].T
     mask_copy.wait()
     others(own_a, GROUP, lambda j: gram_third(j, j).wait_recv())
+    x_begin(PIECES - 1)
     x_end(0)
     x_end(1)
     state_r[...] = sparse_part(state_x[...], (0,), True) - dense_part(state_x[...])
-    x_forward(PIECES - 1)
     x_end(2)
     x_end(3)
 
@@ -367,39 +355,53 @@
     out_begin(0, state_r[...])
     image[...] = dense_part(state_r[...]) + CONFIDENCE * sparse_part(state_r[...], (0, 1), False)
     out_begin(1, image[...])
-    norm_0, curve_0 = all_sums(0, [state_r[...] * state_r[...], state_r[...] * image[...]])
-    alpha_0 = norm_0 / curve_0
-    state_d[...] = state_r[...]
-    state_r[...] = state_r[...] - alpha_0 * image[...]
-
-    image_r = dense_part(state_r[...]) + CONFIDENCE * sparse_part(state_r[...], (0, 1), False)
-    out_begin(2, image_r)
-    norm_1, curve_rr, curve_rd, curve_dr = all_sums(
-        1,
+
+    full = gram[...].reshape(128, 128)
+    diagonal = lax.broadcasted_iota(jnp.int32, full.shape, 0) == lax.broadcasted_iota(jnp.int32, full.shape, 1)
+    trace = jnp.sum(jnp.sum(jnp.where(diagonal, full, 0.0), axis=0, keepdims=True), axis=1, keepdims=True)
+    theta = 1.0 / (trace * (1.0 / 128) + RIDGE)
+    state_d[...] = state_r[...] - theta * image[...]
+    image_w = dense_part(state_d[...]) + CONFIDENCE * sparse_part(state_d[...], (0, 1), False)
+    out_begin(2, image_w)
+    rr, rw, ww, ri, wi, rj, wj = all_sums(
         [
             state_r[...] * state_r[...],
-            state_r[...] * image_r,
+            state_r[...] * state_d[...],
+            state_d[...] * state_d[...],
             state_r[...] * image[...],
-            state_d[...] * image_r,
-        ],
+            state_d[...] * image[...],
+            state_r[...] * image_w,
+            state_d[...] * image_w,
+        ]
     )
-    beta = norm_1 / norm_0
-    alpha_1 = norm_1 / (curve_rr + beta * (curve_rd + curve_dr) + beta * beta * curve_0)
+    delta = rw / (rr - rw)
+    more = 1.0 + delta
+    alpha_0 = theta * more
+    norm_1 = delta * delta * rr - 2.0 * delta * more * rw + more * more * ww
+    beta = norm_1 / rr
+    curve_1 = (
+        more * more * wj
+        - delta * more * (wi + rj)
+        + delta * delta * ri
+        + beta * (more * (wi + rj) - 2.0 * delta * ri)
+        + beta * beta * ri
+    )
+    alpha_1 = norm_1 / curve_1
 
     for index in range(3):
         out_end(index)
     for block in range(blocks):
         lanes = pl.ds((block // 2) * 128, 128)
         for side in range(n_cols // 2):
-            start_r, image_d, image_1 = [
+            start_r, image_r, image_d = [
                 interleave(out_recv[i, 2 * side, :, lanes], out_recv[i, 2 * side + 1, :, lanes], block % 2 == 1)
                 for i in range(3)
             ]
             here = pl.ds(block * 256 + side * 128, 128)
-            mid_r = start_r - alpha_0 * image_d
+            mid_r = more * (start_r - theta * image_r) - delta * start_r
             mid_x = users_ref[:, here] + alpha_0 * start_r
             solution_ref[:, here] = mid_x + alpha_1 * (mid_r + beta * start_r)
-            residual_ref[:, here] = mid_r - alpha_1 * (image_1 + beta * image_d)
+            residual_ref[:, here] = mid_r - alpha_1 * (more * image_d + (beta - delta) * image_r)
 
     others(own_p, PLANE, lambda j: ask_copy(j, own_p).wait_send())
     others(col, n_cols, lambda j: item_copy(j, col).wait_send())
@@ -410,16 +412,14 @@
     for piece in range(PIECES):
         for step in range(last_step + 1):
             for way in range(2):
-                for h in range(2):
+                for h in range(CHUNKS):
                     if z_travels(step, way, h):
                         z_copy(piece, way, step, h).wait_send()
-        others(own_p, PLANE, lambda j: plane_copy(piece, j, own_p).wait_send())
-        x_copy(piece, 0, col, right).wait_send()
-        x_copy(piece, 1, col, left).wait_send()
-        x_copy(piece, 2, left, right).wait_send()
-    for index in range(2):
-        others(own_a, GROUP, lambda j: sums_copy(2 * index, peer_a, j, own_a).wait_send())
-        others(own_b, GROUP, lambda j: sums_copy(2 * index + 1, peer_b, j, own_b).wait_send())
+        for half in range(2):
+            others(own_p, PLANE, lambda j: plane_copy(piece, half, j, own_p).wait_send())
+        others(col, n_cols, lambda j: x_copy(piece, j, col).wait_send())
+    others(own_a, GROUP, lambda j: sums_copy(0, peer_a, j, own_a).wait_send())
+    others(own_b, GROUP, lambda j: sums_copy(1, peer_b, j, own_b).wait_send())
     for index in range(3):
         others(col, n_cols, lambda j: out_copy(index, j, col).wait_send())
 
@@ -441,15 +441,16 @@
     return pl.pallas_call(
         kernel,
         out_shape=(out, out),
-        in_specs=[smem] * 7 + [vmem] * 3 + [pl.BlockSpec(memory_space=pl.ANY)],
+        in_specs=[smem] * 8 + [vmem] * 3 + [pl.BlockSpec(memory_space=pl.ANY)],
         out_specs=(vmem, vmem),
         scratch_shapes=[
             pltpu.VMEM((PLANE, 8, 128), jnp.int32),
             pltpu.VMEM((PLANE, 128), jnp.int32),
             pltpu.SMEM((PLANE, 128), jnp.int32),
-            *[pltpu.VMEM((Z_CHIPS, item_blocks, 16, 128), BF16)] * PIECES,
+            *[pltpu.VMEM((Z_CHIPS - 1, item_blocks, 16, 128), BF16)] * PIECES,
+            *[pltpu.VMEM((item_blocks, 16, 128), BF16)] * PIECES,
             pltpu.VMEM((PIECES, PLANE, SLOTS, 16, 128), BF16),
-            *[pltpu.VMEM((PLANE * SLOTS, 16, 128), BF16)] * PIECES,
+            *[pltpu.VMEM((PLANE, SLOTS, 16, 128), BF16)] * PIECES,
             pltpu.VMEM((2, slots, width, 128), BF16),
             pltpu.VMEM((slots, own_users, tile_cols), BF16),
             pltpu.VMEM((n_cols, col_width, mine), F32),
@@ -460,8 +461,8 @@
             pltpu.VMEM((piece, width), F32),
             pltpu.VMEM((GROUP, piece, width), F32),
             pltpu.VMEM((GROUP, piece, width), F32),
-            pltpu.VMEM((4, 8, 128), F32),
-            pltpu.VMEM((4, GROUP, 8, 128), F32),
+            pltpu.VMEM((2, 1, 128), F32),
+            pltpu.VMEM((2, GROUP, 1, 128), F32),
             pltpu.VMEM((blocks, 2 * own_users, width), BF16),
             pltpu.VMEM((slots, own_users, width), F32),
             pltpu.VMEM((mine, width), F32),
@@ -474,20 +475,20 @@
             dma,
             dma((PLANE,)),
             dma((PLANE,)),
-            dma((PIECES, 2, Z_CHIPS // 2, 2)),
-            dma((PIECES, 2, Z_CHIPS // 2, 2)),
-            dma((PIECES, PLANE)),
-            dma((PIECES, PLANE)),
-            dma((PIECES, 3)),
-            dma((PIECES, 3)),
+            dma((PIECES, 2, Z_CHIPS // 2, CHUNKS)),
+            dma((PIECES, 2, Z_CHIPS // 2, CHUNKS)),
+            dma((PIECES, 2, PLANE)),
+            dma((PIECES, 2, PLANE)),
+            dma((PIECES, n_cols)),
+            dma((PIECES, n_cols)),
             dma((n_cols,)),
             dma((n_cols,)),
             dma((n_cols,)),
             dma((n_cols,)),
             dma((3, GROUP)),
             dma((3, GROUP)),
-            dma((4, GROUP)),
-            dma((4, GROUP)),
+            dma((2, GROUP)),
+            dma((2, GROUP)),
             dma((3, n_cols)),
             dma((3, n_cols)),
         ],
@@ -523,6 +524,8 @@
     rank = jnp.minimum(jnp.sum(earlier.astype(jnp.int32), axis=1), CAPACITY - 1)
     peer = holder // GROUP * CORES + holder % CORES
     distance = (holder // CORES % Z_CHIPS - own_z + Z_CHIPS) % Z_CHIPS
+    far = Z_CHIPS // 2
+    distance = jnp.where(distance == far, Z_CHIPS - 1, distance - (distance > far).astype(jnp.int32))
     raw = jnp.where(live, peer * SLOTS + distance * CAPACITY + rank, 0)
     raw_range = jnp.arange(PLANE * SLOTS, dtype=jnp.int32)
     hits = ((raw[None, :] == raw_range[:, None]) & live[None, :]).astype(jnp.int32)
@@ -530,7 +533,8 @@
     ask = jnp.pad(ask, ((0, 0), (0, 7), (0, 128 - SLOTS)))
     raw_sorted = jnp.sum(chosen * raw[None, :], axis=1)
     return solve(
-        (raw_sorted, perm, user, keep, live_sorted, last, has), ask, user_factors, item_factors, tile_mask, n_cols
+        (raw_sorted // SLOTS, raw_sorted % SLOTS, perm, user, keep, live_sorted, last, has),
+        ask, user_factors, item_factors, tile_mask, n_cols,
     )
 
 

time: 144 us -> 127 us (0.88)
  Pallas kernels: 136 us -> 119 us
    pallas_call x1, Pallas kernels: 136 us -> 119 us  [solve(): pl.pallas_call(kernel, out_shape=(out, out), in_specs=[smem] * 8 + [vmem]...]
where the time goes in v3:
time: 127 us
  Pallas kernels  119 us (94%)
  local copies, waits for them, and re-layouts  3.48 us (3%)
  other arithmetic  3.06 us (2%)
  between operations  1.36 us (1%)
    pallas_call x1, Pallas kernels, solve(): pl.pallas_call(kernel, out_shape=(out, out), in_specs=[smem] * 8 + [vmem]...  119 us
    unnamed x6, local copies, waits for them, and re-layouts  3.39 us

profile of v3, /device:TPU:1, one launch (start us, length us, event | category | flops | bytes accessed | tf_op | source)
XLA Modules:
  0.0 126.9 jit_solution(11721895872234771320)
XLA Ops:
  1.3 0.7 and_select_fusion
  2.0 0.2 convert_reduce_fusion
  2.2 0.7 iota_add_fusion
  2.9 0.2 convert_reduce_fusion.1
  3.0 0.1 select_reduce_fusion
  3.2 0.8 select_reduce_fusion.1
  4.0 0.1 select_reduce_fusion.4.last_ref
  4.1 0.1 fusion.4
  4.2 0.1 slice_compare_fusion
  4.3 0.1 add_convert_fusion.keep_ref
  4.4 0.1 reshape.20
  4.5 0.0 copy-start
  4.5 1.0 copy-done
  5.5 0.0 copy-start.1
  5.5 0.9 copy-done.1
  6.5 119.0 %shard_map.77 = (f32[32,2048]{1,0:T(8,128)S(1)}, f32[32,2048]{1,0:T(8,128)S(1)}) custom-call(s32[72]{0:T(128)S(1)} %get-tuple-element.8.holder_ref, s32[72]{0:T(128)S(1)} %get-tuple-element.7.place_ref, s32[72]{0:T(128)S(1)} %get-tuple-element.3.perm_ref, s32[72]{0:T(128)S(1)} %get-tuple-element.2.user_ref, f32[72]{0:T(128)S(1)} %add_convert_fusion.keep_ref, ...), custom_call_target="tpu_custom_call" | custom-call | tf_op jit(solution)/shard_map/pallas_call | solution.py:441
  125.5 0.7 copy.13
  126.2 0.7 copy.14
  (5 shorter events, 0.0 us)
Async XLA Ops:
  4.5 1.0 copy-start
  5.5 0.9 copy-start.1

commit v4 on v3

--- a/solution.py
+++ b/solution.py
@@ -33,14 +33,13 @@
 
 
 def kernel(
-    holder_ref, place_ref, perm_ref, user_ref, keep_ref, live_ref, last_ref, has_ref,
-    ask_ref, users_ref, items_ref, mask_ref,
+    count_ref, user_in, item_in, users_in, items_in, mask_ref,
     solution_ref, residual_ref,
-    asked, asked_rows, asked_smem, ring_0, ring_1, ring_2, ring_3, far_0, far_1, far_2, far_3, plane_send,
+    users_ref, items_ref, user_col, item_col, table, table_smem, ask, asked, asked_rows, asked_smem, ring_0, ring_1, ring_2, ring_3, far_0, far_1, far_2, far_3, plane_send,
     plane_recv_0, plane_recv_1, plane_recv_2, plane_recv_3, tiles, masks,
     users_send, users_recv, items_recv, gram_part, gram_recv, gram_piece, gram_all, gram,
     sums_send, sums_recv, halves, terms, state_x, state_r, state_d, image, out_send, out_recv,
-    mask_sem, smem_sem, a_send, a_recv, z_send, z_recv, y_send, y_recv, x_send, x_recv,
+    users_sem, items_sem, mask_sem, smem_sem, table_sem, a_send, a_recv, z_send, z_recv, y_send, y_recv, x_send, x_recv,
     u_send, u_recv, i_send, i_recv, g_send, g_recv, s_send, s_recv, o_send, o_recv,
 ):
     rings = (ring_0, ring_1, ring_2, ring_3)
@@ -78,6 +77,10 @@
         (own_y * GROUP + lax.rem(own_z + step, Z_CHIPS) * CORES + core, col) for step in (1, Z_CHIPS - 1)
     ]
 
+    right, left = lax.rem(col + 1, n_cols), lax.rem(col + n_cols - 1, n_cols)
+    across = lax.rem(col + 2, n_cols)
+    half_slots = tile_total // 2
+
     def others(own, count, body):
         def step(i, carry):
             body(lax.rem(own + i, count))
@@ -90,6 +93,10 @@
             src_ref=src, dst_ref=dst, send_sem=send_sem, recv_sem=recv_sem, device_id=peer, device_id_type=MESH
         )
 
+    items_copy = pltpu.make_async_copy(items_in, items_ref, items_sem)
+    users_copy = pltpu.make_async_copy(users_in, users_ref, users_sem)
+    items_copy.start()
+    users_copy.start()
     mask_copy = pltpu.make_async_copy(
         mask_ref.at[:, pl.ds(pl.multiple_of(col * own_users, own_users), own_users), :], masks, mask_sem
     )
@@ -111,7 +118,9 @@
             rings[piece][0, b] = block[16 * sub : 16 * sub + 16, 128 * lane : 128 * lane + 128]
         return carry
 
+    items_copy.wait()
     lax.fori_loop(0, item_blocks, split_items, 0, unroll=4)
+    users_copy.wait()
     for dest in range(n_cols):
         for pair in range(blocks // 2):
             at = (dest // 2) * 128
@@ -119,6 +128,54 @@
             second = users_ref[:, pl.ds((2 * pair + 1) * 256 + at, 128)]
             users_send[dest, :, pl.ds(pair * 128, 128)] = interleave(first, second, dest % 2 == 1)
     pl.semaphore_wait(barrier, 2 * (GROUP - 1) + Y_CHIPS - 1)
+
+    def make_tables():
+        user_col[...] = jnp.zeros_like(user_col)
+        item_col[...] = jnp.zeros_like(item_col)
+
+        def fill(t, carry):
+            user_col[pl.ds(t, 1), :] = jnp.full((1, 128), user_in[t], jnp.int32)
+            item_col[pl.ds(t, 1), :] = jnp.full((1, 128), item_in[t], jnp.int32)
+            return carry
+
+        lax.fori_loop(0, tile_total, fill, 0, unroll=8)
+        square = user_col.shape
+        down = lax.broadcasted_iota(jnp.int32, square, 0)
+        over = lax.broadcasted_iota(jnp.int32, square, 1)
+        count = count_ref[0]
+        live = down < count
+        users_down, items_down = user_col[...], item_col[...]
+
+        def total(cond, value, axis):
+            return jnp.sum(jnp.where(cond, value, 0), axis=axis, keepdims=True)
+
+        key = jnp.where(live, users_down, blocks) * 128 + down
+        place = total(key.T < key, 1, 1)
+        chosen = place == over
+        holder = items_down // item_blocks
+        earlier = (holder.T == holder) & (over < down) & (over < count)
+        rank = jnp.minimum(total(earlier, 1, 1), CAPACITY - 1)
+        peer = holder // GROUP * CORES + holder % CORES
+        distance = (holder // CORES % Z_CHIPS - own_z + Z_CHIPS) % Z_CHIPS
+        far = Z_CHIPS // 2
+        distance = jnp.where(distance == far, Z_CHIPS - 1, jnp.where(distance > far, distance - 1, distance))
+        raw = jnp.where(live, peer * SLOTS + distance * CAPACITY + rank, 0)
+        ask[...] = total((raw == over) & live, items_down % item_blocks, 0)
+        user = total(chosen, users_down, 0)
+        up_to = total(live & (users_down <= over), 1, 0)
+        lane = over[:1]
+        rows = [
+            total(chosen, raw, 0),
+            total(chosen, down, 0),
+            user,
+            jnp.where((user == pltpu.roll(user, 1, 1)) & (lane > 0), 1, 0),
+            jnp.where(lane < count, 1, 0),
+            jnp.maximum(up_to - 1, 0),
+            total(live & (users_down == over), 1, 0),
+            jnp.zeros_like(user),
+        ]
+        table[...] = jnp.concatenate(rows, axis=0)
+        pltpu.make_async_copy(table, table_smem, table_sem).start()
 
     def z_copy(piece, way, step, h):
         chunk = pl.ds(part * h, part)
@@ -147,7 +204,7 @@
                     z_copy(piece, way, step, h).start()
 
     def ask_copy(j, slot):
-        return remote(ask_ref.at[j], asked.at[slot], a_send.at[j], a_recv.at[slot], peer_p(j))
+        return remote(ask, asked.at[slot], a_send.at[j], a_recv.at[slot], peer_p(j))
 
     def plane_copy(piece, half, j, slot):
         first, count = ((0, NEAR), (NEAR, CAPACITY))[half]
@@ -162,9 +219,9 @@
         def pick(j, carry):
             for slot in range(first, first + count):
                 if half == 0:
-                    block = rings[piece][slot // CAPACITY, asked_smem[j, slot]]
+                    block = rings[piece][slot // CAPACITY, asked_smem[j, own_p * SLOTS + slot]]
                 else:
-                    block = fars[piece][asked_smem[j, slot]]
+                    block = fars[piece][asked_smem[j, own_p * SLOTS + slot]]
                 plane_send[piece, j, slot] = block
             return carry
 
@@ -172,14 +229,11 @@
         others(own_p, PLANE, lambda j: plane_copy(piece, half, j, own_p).start())
         plane_recvs[piece][own_p, pl.ds(first, count)] = plane_send[piece, own_p, pl.ds(first, count)]
 
-    def x_ref(piece, owner):
+    def x_copy(piece, kind, owner, peer):
+        half = (0, 1, 0, 1, 0, 1)[kind]
         rows_at = pl.multiple_of(owner * col_width + 16 * (piece % 2), 16)
-        return tiles.at[piece // 2, :, pl.ds(rows_at, 16), :]
-
-    def x_copy(piece, j, slot):
-        return remote(
-            x_ref(piece, slot), x_ref(piece, slot), x_send.at[piece, j], x_recv.at[piece, slot], peer_c(j)
-        )
+        at = tiles.at[piece // 2, pl.ds(half * half_slots, half_slots), pl.ds(rows_at, 16), :]
+        return remote(at, at, x_send.at[piece, kind], x_recv.at[piece, kind], (row, peer))
 
     def x_begin(piece):
         for half in range(2):
@@ -187,14 +241,25 @@
         rows_at = pl.multiple_of(col * col_width + 16 * (piece % 2), 16)
 
         def pack(s, carry):
-            tiles[piece // 2, s, pl.ds(rows_at, 16), :] = plane_recvs[piece][holder_ref[s], place_ref[s]]
+            raw = table_smem[0, s]
+            tiles[piece // 2, s, pl.ds(rows_at, 16), :] = plane_recvs[piece][raw >> 4, raw & (SLOTS - 1)]
             return carry
 
         lax.fori_loop(0, tile_total, pack, 0, unroll=8)
-        others(col, n_cols, lambda j: x_copy(piece, j, col).start())
+        for kind, peer in ((0, right), (3, left), (1, right), (2, left)):
+            x_copy(piece, kind, col, peer).start()
+
+    def x_forward(piece):
+        x_copy(piece, 0, left, right).wait_recv()
+        x_copy(piece, 4, left, right).start()
+        x_copy(piece, 3, right, left).wait_recv()
+        x_copy(piece, 5, right, left).start()
 
     def x_end(piece):
-        others(col, n_cols, lambda j: x_copy(piece, j, j).wait_recv())
+        x_copy(piece, 1, left, right).wait_recv()
+        x_copy(piece, 2, right, left).wait_recv()
+        x_copy(piece, 4, across, left).wait_recv()
+        x_copy(piece, 5, across, left).wait_recv()
 
     own_cols = pl.ds(pl.multiple_of(col * col_width, col_width), col_width)
 
@@ -248,12 +313,12 @@
         def step(s, running):
             if len(lanes) == 2:
                 item = jnp.concatenate([tiles[0, s], tiles[1, s]], axis=1)
-                mask = masks[perm_ref[s]]
+                mask = masks[table_smem[1, s]]
             else:
                 item = tiles[lanes[0], s]
-                mask = masks[perm_ref[s], :, pl.ds(128 * lanes[0], 128)]
-            mask = mask.astype(F32) * live_ref[s]
-            scores = jnp.dot(halves[user_ref[s]], item, preferred_element_type=F32)
+                mask = masks[table_smem[1, s], :, pl.ds(128 * lanes[0], 128)]
+            mask = mask.astype(F32) * table_smem[4, s].astype(F32)
+            scores = jnp.dot(halves[table_smem[2, s]], item, preferred_element_type=F32)
             scores = scores[:own_users] + scores[own_users:]
             if first_time:
                 strengths = mask * ((1.0 + CONFIDENCE) - CONFIDENCE * scores)
@@ -265,12 +330,12 @@
                 jnp.concatenate([s_high, s_low], axis=0), item, (((1,), (1,)), ((), ())),
                 preferred_element_type=F32,
             )
-            running = both[:own_users] + both[own_users:] + keep_ref[s] * running
+            running = both[:own_users] + both[own_users:] + table_smem[3, s].astype(F32) * running
             terms[s] = running
             return running
 
         lax.fori_loop(0, tile_total, step, jnp.zeros((own_users, 128), F32), unroll=UNROLL)
-        return jnp.concatenate([terms[last_ref[b]] * has_ref[b] for b in range(blocks)], axis=0)
+        return jnp.concatenate([jnp.where(table_smem[6, b] > 0, terms[table_smem[5, b]], 0.0) for b in range(blocks)], axis=0)
 
     def dense_part(vectors):
         return (
@@ -309,8 +374,9 @@
         others(col, n_cols, lambda j: out_copy(index, j, j).wait_recv())
 
     z_step(0, 0)
+    make_tables()
     others(own_p, PLANE, lambda j: ask_copy(j, own_p).start())
-    asked[own_p] = ask_ref[own_p]
+    asked[own_p] = ask[...]
     others(col, n_cols, lambda j: item_copy(j, col).start())
     others(col, n_cols, lambda j: user_copy(j, col).start())
     items_recv[own_cols, :] = item_quarter_ref(col)[...]
@@ -321,6 +387,7 @@
     to_smem = pltpu.make_async_copy(asked_rows, asked_smem, smem_sem)
     to_smem.start()
     to_smem.wait()
+    pltpu.make_async_copy(table, table_smem, table_sem).wait()
 
     span = last_step + 2
     for time in range(1, 2 * (PIECES - 1) + span):
@@ -334,6 +401,8 @@
                     plane_begin(piece, 1)
             if step == span:
                 x_begin(piece)
+            if step == span + 1:
+                x_forward(piece)
         if time == 2:
             gram_1()
         if time == 4:
@@ -348,6 +417,7 @@
     x_end(0)
     x_end(1)
     state_r[...] = sparse_part(state_x[...], (0,), True) - dense_part(state_x[...])
+    x_forward(PIECES - 1)
     x_end(2)
     x_end(3)
 
@@ -417,14 +487,16 @@
                         z_copy(piece, way, step, h).wait_send()
         for half in range(2):
             others(own_p, PLANE, lambda j: plane_copy(piece, half, j, own_p).wait_send())
-        others(col, n_cols, lambda j: x_copy(piece, j, col).wait_send())
+        for kind, owner, peer in ((0, col, right), (1, col, right), (2, col, left), (3, col, left), (4, left, right), (5, right, left)):
+            x_copy(piece, kind, owner, peer).wait_send()
     others(own_a, GROUP, lambda j: sums_copy(0, peer_a, j, own_a).wait_send())
     others(own_b, GROUP, lambda j: sums_copy(1, peer_b, j, own_b).wait_send())
     for index in range(3):
         others(col, n_cols, lambda j: out_copy(index, j, col).wait_send())
 
 
-def solve(tables, ask, user_factors, item_factors, tile_mask, n_cols):
+def on_device(user_factors, item_factors, tile_user, tile_item, tile_count, tile_mask):
+    n_cols = lax.axis_size("cols")
     col_width, users = user_factors.shape
     slots, tile_rows, tile_cols = tile_mask.shape
     width = col_width * n_cols
@@ -435,16 +507,24 @@
     item_quarter = item_factors.shape[1] // n_cols
     vmem = pl.BlockSpec(memory_space=pltpu.VMEM)
     smem = pl.BlockSpec(memory_space=pltpu.SMEM)
+    hbm = pl.BlockSpec(memory_space=pl.ANY)
     piece = width // GROUP
     out = jax.ShapeDtypeStruct((col_width, users), F32)
     dma = pltpu.SemaphoreType.DMA
     return pl.pallas_call(
         kernel,
         out_shape=(out, out),
-        in_specs=[smem] * 8 + [vmem] * 3 + [pl.BlockSpec(memory_space=pl.ANY)],
+        in_specs=[smem] * 3 + [hbm] * 3,
         out_specs=(vmem, vmem),
         scratch_shapes=[
-            pltpu.VMEM((PLANE, 8, 128), jnp.int32),
+            pltpu.VMEM((col_width, users), F32),
+            pltpu.VMEM((col_width, item_factors.shape[1]), BF16),
+            pltpu.VMEM((128, 128), jnp.int32),
+            pltpu.VMEM((128, 128), jnp.int32),
+            pltpu.VMEM((8, 128), jnp.int32),
+            pltpu.SMEM((8, 128), jnp.int32),
+            pltpu.VMEM((1, 128), jnp.int32),
+            pltpu.VMEM((PLANE, 1, 128), jnp.int32),
             pltpu.VMEM((PLANE, 128), jnp.int32),
             pltpu.SMEM((PLANE, 128), jnp.int32),
             *[pltpu.VMEM((Z_CHIPS - 1, item_blocks, 16, 128), BF16)] * PIECES,
@@ -473,14 +553,17 @@
             pltpu.VMEM((3, n_cols, col_width, mine), F32),
             dma,
             dma,
+            dma,
+            dma,
+            dma,
             dma((PLANE,)),
             dma((PLANE,)),
             dma((PIECES, 2, Z_CHIPS // 2, CHUNKS)),
             dma((PIECES, 2, Z_CHIPS // 2, CHUNKS)),
             dma((PIECES, 2, PLANE)),
             dma((PIECES, 2, PLANE)),
-            dma((PIECES, n_cols)),
-            dma((PIECES, n_cols)),
+            dma((PIECES, 6)),
+            dma((PIECES, 6)),
             dma((n_cols,)),
             dma((n_cols,)),
             dma((n_cols,)),
@@ -495,47 +578,7 @@
         compiler_params=pltpu.CompilerParams(
             collective_id=0, has_side_effects=True, vmem_limit_bytes=VMEM_BYTES
         ),
-    )(*tables, ask, user_factors, item_factors, tile_mask)
-
-
-def on_device(user_factors, item_factors, tile_user, tile_item, tile_count, tile_mask):
-    n_cols = lax.axis_size("cols")
-    tile_rows = tile_mask.shape[1]
-    slots = tile_user.shape[0]
-    blocks = user_factors.shape[1] // tile_rows
-    item_blocks = item_factors.shape[1] // tile_rows
-    own_z = lax.axis_index("rows") // CORES % Z_CHIPS
-
-    order = jnp.arange(slots, dtype=jnp.int32)
-    live = order < tile_count[0]
-    key = jnp.where(live, tile_user, blocks) * slots + order
-    place = jnp.sum((key[None, :] < key[:, None]).astype(jnp.int32), axis=1)
-    chosen = (place[None, :] == order[:, None]).astype(jnp.int32)
-    perm = jnp.sum(chosen * order[None, :], axis=1)
-    user = jnp.sum(chosen * tile_user[None, :], axis=1)
-    live_sorted = live.astype(F32)
-    keep = jnp.concatenate([jnp.zeros((1,), F32), (user[1:] == user[:-1]).astype(F32)])
-    per_block = (user[None, :] == jnp.arange(blocks, dtype=jnp.int32)[:, None]) & live[None, :]
-    has = jnp.any(per_block, axis=1).astype(F32)
-    last = jnp.max(jnp.where(per_block, order[None, :], 0), axis=1)
-
-    holder = tile_item // item_blocks
-    earlier = (holder[None, :] == holder[:, None]) & (order[None, :] < order[:, None]) & live[None, :]
-    rank = jnp.minimum(jnp.sum(earlier.astype(jnp.int32), axis=1), CAPACITY - 1)
-    peer = holder // GROUP * CORES + holder % CORES
-    distance = (holder // CORES % Z_CHIPS - own_z + Z_CHIPS) % Z_CHIPS
-    far = Z_CHIPS // 2
-    distance = jnp.where(distance == far, Z_CHIPS - 1, distance - (distance > far).astype(jnp.int32))
-    raw = jnp.where(live, peer * SLOTS + distance * CAPACITY + rank, 0)
-    raw_range = jnp.arange(PLANE * SLOTS, dtype=jnp.int32)
-    hits = ((raw[None, :] == raw_range[:, None]) & live[None, :]).astype(jnp.int32)
-    ask = jnp.sum(hits * (tile_item % item_blocks)[None, :], axis=1).reshape(PLANE, 1, SLOTS)
-    ask = jnp.pad(ask, ((0, 0), (0, 7), (0, 128 - SLOTS)))
-    raw_sorted = jnp.sum(chosen * raw[None, :], axis=1)
-    return solve(
-        (raw_sorted // SLOTS, raw_sorted % SLOTS, perm, user, keep, live_sorted, last, has),
-        ask, user_factors, item_factors, tile_mask, n_cols,
-    )
+    )(tile_count, tile_user, tile_item, user_factors, item_factors, tile_mask)
 
 
 def solution(mesh):

time: 127 us -> 116 us (0.913)
  Pallas kernels: 119 us -> 110 us
  other arithmetic: 3.06 us -> 0 us
    pallas_call x1, Pallas kernels: 119 us -> 110 us  [on_device(): pl.pallas_call(kernel, out_shape=(out, out), in_specs=[smem] * 3 + [hbm]...]
    unnamed x6 -> x10, local copies, waits for them, and re-layouts: 3.39 us -> 4.7 us
    reduce_sum x4 -> x0, other arithmetic: 1.27 us -> none  [the longest x1 0.81 us: on_device(): user = jnp.sum(chosen * tile_user[None, :], axis=1)]
where the time goes in v4:
time: 116 us
  Pallas kernels  110 us (95%)
  local copies, waits for them, and re-layouts  4.7 us (4%)
  between operations  1.3 us (1%)
    pallas_call x1, Pallas kernels, on_device(): pl.pallas_call(kernel, out_shape=(out, out), in_specs=[smem] * 3 + [hbm]...  110 us
    unnamed x10, local copies, waits for them, and re-layouts  4.7 us

profile of v4, /device:TPU:1, one launch (start us, length us, event | category | flops | bytes accessed | tf_op | source)
XLA Modules:
  0.0 115.8 jit_solution(8835425354128735257)
XLA Ops:
  1.3 0.0 copy-start
  1.3 1.0 copy-done
  2.3 0.0 copy-start.1
  2.3 0.9 copy-done.1
  3.3 0.0 copy-start.2
  3.3 0.7 copy-done.2
  3.9 0.0 copy-start.3
  3.9 0.7 copy-done.3
  4.6 109.8 %shard_map.77 = (f32[32,2048]{1,0:T(8,128)S(1)}, f32[32,2048]{1,0:T(8,128)S(1)}) custom-call(s32[1]{0:T(128)S(6)} %copy.10.count_ref, s32[72]{0:T(128)S(1)} %copy-done.2, s32[72]{0:T(128)S(1)} %copy-done.3, f32[32,2048]{1,0:T(8,128)S(1)} %copy-done.1, bf16[32,8192]{1,0:T(8,128)(2,1)S(1)} %copy-done, bf16[72,256,256]{2,1,0:T(8,128)(2,1)} %mask_ref.1), custom_call_target="tpu_custom_call" | custom-call | tf_op jit(solution)/shard_map/pallas_call | solution.py:514
  114.4 0.7 copy.11
  115.1 0.7 copy.12
Async XLA Ops:
  1.3 1.0 copy-start
  2.3 0.9 copy-start.1
  3.3 0.7 copy-start.2
  3.9 0.7 copy-start.3

commit v5 on v4

--- a/solution.py
+++ b/solution.py
@@ -1,3 +1,5 @@
+import functools
+
 import jax
 import jax.numpy as jnp
 from jax import lax
@@ -21,8 +23,11 @@
 PIECES = 4
 CHUNKS = 4
 NEAR = SLOTS - CAPACITY
-UNROLL = 24
-VMEM_BYTES = 48 * 1024 * 1024
+UNROLL = 36
+VMEM_BYTES = 56 * 1024 * 1024
+STARTS = (0, 2, 4, 6)
+PACK_AFTER = -0.5
+PASS_AFTER = 0.5
 
 
 def interleave(first, second, odd):
@@ -33,13 +38,13 @@
 
 
 def kernel(
-    count_ref, user_in, item_in, users_in, items_in, mask_ref,
-    solution_ref, residual_ref,
-    users_ref, items_ref, user_col, item_col, table, table_smem, ask, asked, asked_rows, asked_smem, ring_0, ring_1, ring_2, ring_3, far_0, far_1, far_2, far_3, plane_send,
+    count_hbm, user_hbm, item_hbm, users_in, items_in, mask_ref,
+    vectors_ref, scalars_ref,
+    count_ref, user_in, item_in, users_ref, items_ref, user_col, item_col, table, table_smem, ask, asked, asked_rows, asked_smem, ring_0, ring_1, ring_2, ring_3, far_0, far_1, far_2, far_3, plane_send,
     plane_recv_0, plane_recv_1, plane_recv_2, plane_recv_3, tiles, masks,
     users_send, users_recv, items_recv, gram_part, gram_recv, gram_piece, gram_all, gram,
     sums_send, sums_recv, halves, terms, state_x, state_r, state_d, image, out_send, out_recv,
-    users_sem, items_sem, mask_sem, smem_sem, table_sem, a_send, a_recv, z_send, z_recv, y_send, y_recv, x_send, x_recv,
+    lists_sem, users_sem, items_sem, mask_sem, smem_sem, table_sem, a_send, a_recv, z_send, z_recv, y_send, y_recv, x_send, x_recv,
     u_send, u_recv, i_send, i_recv, g_send, g_recv, s_send, s_recv, o_send, o_recv,
 ):
     rings = (ring_0, ring_1, ring_2, ring_3)
@@ -97,19 +102,25 @@
     users_copy = pltpu.make_async_copy(users_in, users_ref, users_sem)
     items_copy.start()
     users_copy.start()
+    list_copies = [
+        pltpu.make_async_copy(src, dst, lists_sem.at[i])
+        for i, (src, dst) in enumerate(((count_hbm, count_ref), (user_hbm, user_in), (item_hbm, item_in)))
+    ]
+    for copy in list_copies:
+        copy.start()
     mask_copy = pltpu.make_async_copy(
         mask_ref.at[:, pl.ds(pl.multiple_of(col * own_users, own_users), own_users), :], masks, mask_sem
     )
-    mask_copy.start()
 
     barrier = pltpu.get_barrier_semaphore()
 
     def greet(peer):
         pl.semaphore_signal(barrier, inc=1, device_id=peer, device_id_type=MESH)
 
-    others(own_a, GROUP, lambda j: greet(peer_a(j)))
-    others(own_b, GROUP, lambda j: greet(peer_b(j)))
-    others(own_y, Y_CHIPS, lambda j: greet(peer_p(j * CORES + 1 - core)))
+    for peer in z_peers:
+        greet(peer)
+    others(own_p, PLANE, lambda j: greet(peer_p(j)))
+    others(col, n_cols, lambda j: greet(peer_c(j)))
 
     def split_items(b, carry):
         block = items_ref[:, pl.ds(pl.multiple_of(b * 256, 256), 256)]
@@ -120,15 +131,6 @@
 
     items_copy.wait()
     lax.fori_loop(0, item_blocks, split_items, 0, unroll=4)
-    users_copy.wait()
-    for dest in range(n_cols):
-        for pair in range(blocks // 2):
-            at = (dest // 2) * 128
-            first = users_ref[:, pl.ds(2 * pair * 256 + at, 128)]
-            second = users_ref[:, pl.ds((2 * pair + 1) * 256 + at, 128)]
-            users_send[dest, :, pl.ds(pair * 128, 128)] = interleave(first, second, dest % 2 == 1)
-    pl.semaphore_wait(barrier, 2 * (GROUP - 1) + Y_CHIPS - 1)
-
     def make_tables():
         user_col[...] = jnp.zeros_like(user_col)
         item_col[...] = jnp.zeros_like(item_col)
@@ -177,6 +179,18 @@
         table[...] = jnp.concatenate(rows, axis=0)
         pltpu.make_async_copy(table, table_smem, table_sem).start()
 
+    for copy in list_copies:
+        copy.wait()
+    make_tables()
+    users_copy.wait()
+    for dest in range(n_cols):
+        for pair in range(blocks // 2):
+            at = (dest // 2) * 128
+            first = users_ref[:, pl.ds(2 * pair * 256 + at, 128)]
+            second = users_ref[:, pl.ds((2 * pair + 1) * 256 + at, 128)]
+            users_send[dest, :, pl.ds(pair * 128, 128)] = interleave(first, second, dest % 2 == 1)
+    pl.semaphore_wait(barrier, 2 + PLANE - 1 + n_cols - 1)
+
     def z_copy(piece, way, step, h):
         chunk = pl.ds(part * h, part)
         if way == 0:
@@ -374,50 +388,55 @@
         others(col, n_cols, lambda j: out_copy(index, j, j).wait_recv())
 
     z_step(0, 0)
-    make_tables()
+    mask_copy.start()
     others(own_p, PLANE, lambda j: ask_copy(j, own_p).start())
     asked[own_p] = ask[...]
     others(col, n_cols, lambda j: item_copy(j, col).start())
+    z_step(0, 1)
     others(col, n_cols, lambda j: user_copy(j, col).start())
     items_recv[own_cols, :] = item_quarter_ref(col)[...]
     users_recv[own_cols, :] = users_send[col]
 
-    others(own_p, PLANE, lambda j: ask_copy(j, j).wait_recv())
-    asked_rows[...] = asked[:, 0, :]
-    to_smem = pltpu.make_async_copy(asked_rows, asked_smem, smem_sem)
-    to_smem.start()
-    to_smem.wait()
-    pltpu.make_async_copy(table, table_smem, table_sem).wait()
+    def asked_ready():
+        others(own_p, PLANE, lambda j: ask_copy(j, j).wait_recv())
+        asked_rows[...] = asked[:, 0, :]
+        to_smem = pltpu.make_async_copy(asked_rows, asked_smem, smem_sem)
+        to_smem.start()
+        to_smem.wait()
+        pltpu.make_async_copy(table, table_smem, table_sem).wait()
 
     span = last_step + 2
-    for time in range(1, 2 * (PIECES - 1) + span):
-        for piece in range(PIECES):
-            step = time - 2 * piece
-            if 0 <= step < span:
-                z_step(piece, step)
-                if step == span - 2:
-                    plane_begin(piece, 0)
-                if step == span - 1:
-                    plane_begin(piece, 1)
-            if step == span:
-                x_begin(piece)
-            if step == span + 1:
-                x_forward(piece)
-        if time == 2:
-            gram_1()
-        if time == 4:
-            gram_2()
-        if time == 5:
-            gram_3()
-    others(col, n_cols, lambda j: user_copy(j, j).wait_recv())
-    state_x[...] = users_recv[...].T
-    mask_copy.wait()
-    others(own_a, GROUP, lambda j: gram_third(j, j).wait_recv())
-    x_begin(PIECES - 1)
-    x_end(0)
-    x_end(1)
-    state_r[...] = sparse_part(state_x[...], (0,), True) - dense_part(state_x[...])
-    x_forward(PIECES - 1)
+    def first_half():
+        others(col, n_cols, lambda j: user_copy(j, j).wait_recv())
+        state_x[...] = users_recv[...].T
+        mask_copy.wait()
+        others(own_a, GROUP, lambda j: gram_third(j, j).wait_recv())
+        x_end(1)
+        state_r[...] = sparse_part(state_x[...], (0,), True) - dense_part(state_x[...])
+
+    def gram_middle():
+        x_end(0)
+        gram_2()
+
+    events = []
+    for piece, start in enumerate(STARTS):
+        for step in range(span):
+            if (piece, step) not in ((0, 0), (0, 1)):
+                events.append((start + step, functools.partial(z_step, piece, step)))
+            if step == span - 2:
+                if piece == 0:
+                    events.append((start + step, asked_ready))
+                events.append((start + step, functools.partial(plane_begin, piece, 0)))
+            if step == span - 1:
+                events.append((start + step, functools.partial(plane_begin, piece, 1)))
+        events.append((start + span + PACK_AFTER, functools.partial(x_begin, piece)))
+        events.append((start + span + PASS_AFTER, functools.partial(x_forward, piece)))
+    events.append((STARTS[0] + span, gram_1))
+    events.append((STARTS[0] + span + 2, gram_middle))
+    events.append((STARTS[-1] + span, gram_3))
+    events.append((STARTS[-1] + span, first_half))
+    for _, event in sorted(events, key=lambda item: item[0]):
+        event()
     x_end(2)
     x_end(3)
 
@@ -463,15 +482,13 @@
     for block in range(blocks):
         lanes = pl.ds((block // 2) * 128, 128)
         for side in range(n_cols // 2):
-            start_r, image_r, image_d = [
-                interleave(out_recv[i, 2 * side, :, lanes], out_recv[i, 2 * side + 1, :, lanes], block % 2 == 1)
-                for i in range(3)
-            ]
             here = pl.ds(block * 256 + side * 128, 128)
-            mid_r = more * (start_r - theta * image_r) - delta * start_r
-            mid_x = users_ref[:, here] + alpha_0 * start_r
-            solution_ref[:, here] = mid_x + alpha_1 * (mid_r + beta * start_r)
-            residual_ref[:, here] = mid_r - alpha_1 * (more * image_d + (beta - delta) * image_r)
+            for i in range(3):
+                vectors_ref[i, :, here] = interleave(
+                    out_recv[i, 2 * side, :, lanes], out_recv[i, 2 * side + 1, :, lanes], block % 2 == 1
+                )
+    for i, value in enumerate((theta, delta, alpha_0, alpha_1, beta)):
+        scalars_ref[i : i + 1, :] = jnp.broadcast_to(value, (1, 128))
 
     others(own_p, PLANE, lambda j: ask_copy(j, own_p).wait_send())
     others(col, n_cols, lambda j: item_copy(j, col).wait_send())
@@ -506,17 +523,21 @@
     mine = blocks * own_users
     item_quarter = item_factors.shape[1] // n_cols
     vmem = pl.BlockSpec(memory_space=pltpu.VMEM)
-    smem = pl.BlockSpec(memory_space=pltpu.SMEM)
     hbm = pl.BlockSpec(memory_space=pl.ANY)
     piece = width // GROUP
-    out = jax.ShapeDtypeStruct((col_width, users), F32)
     dma = pltpu.SemaphoreType.DMA
-    return pl.pallas_call(
+    vectors, scalars = pl.pallas_call(
         kernel,
-        out_shape=(out, out),
-        in_specs=[smem] * 3 + [hbm] * 3,
+        out_shape=(
+            jax.ShapeDtypeStruct((3, col_width, users), F32),
+            jax.ShapeDtypeStruct((8, 128), F32),
+        ),
+        in_specs=[hbm] * 6,
         out_specs=(vmem, vmem),
         scratch_shapes=[
+            pltpu.SMEM(tile_count.shape, jnp.int32),
+            pltpu.SMEM(tile_user.shape, jnp.int32),
+            pltpu.SMEM(tile_item.shape, jnp.int32),
             pltpu.VMEM((col_width, users), F32),
             pltpu.VMEM((col_width, item_factors.shape[1]), BF16),
             pltpu.VMEM((128, 128), jnp.int32),
@@ -551,6 +572,7 @@
             pltpu.VMEM((mine, width), F32),
             pltpu.VMEM((3, n_cols, col_width, mine), F32),
             pltpu.VMEM((3, n_cols, col_width, mine), F32),
+            dma((3,)),
             dma,
             dma,
             dma,
@@ -579,6 +601,13 @@
             collective_id=0, has_side_effects=True, vmem_limit_bytes=VMEM_BYTES
         ),
     )(tile_count, tile_user, tile_item, user_factors, item_factors, tile_mask)
+    start_r, image_r, image_w = vectors[0], vectors[1], vectors[2]
+    theta, delta, alpha_0, alpha_1, beta = [scalars[i, 0] for i in range(5)]
+    more = 1.0 + delta
+    mid_r = more * (start_r - theta * image_r) - delta * start_r
+    solution_field = user_factors + alpha_0 * start_r + alpha_1 * (mid_r + beta * start_r)
+    residual = mid_r - alpha_1 * (more * image_w + (beta - delta) * image_r)
+    return solution_field, residual
 
 
 def solution(mesh):

time: 116 us -> 124 us (1.069)
  other arithmetic: 0 us -> 8.67 us
  local copies, waits for them, and re-layouts: 4.7 us -> 1.44 us
  between operations: 1.3 us -> 3.26 us
    add x0 -> x1, other arithmetic: none -> 4.96 us  [on_device(): user_factors + alpha_0 * start_r + alpha_1 * (mid_r + beta * start_r)]
    unnamed x10 -> x2, local copies, waits for them, and re-layouts: 4.7 us -> 0.01 us
    sub x0 -> x1, other arithmetic: none -> 3.71 us  [on_device(): residual = mid_r - alpha_1 * (more * image_w + (beta - delta) * image_r)]
    slice x0 -> x1, local copies, waits for them, and re-layouts: none -> 1.44 us  [on_device(): theta, delta, alpha_0, alpha_1, beta = [scalars[i, 0] for i in range(5)]]
where the time goes in v5:
time: 124 us
  Pallas kernels  110 us (89%)
  other arithmetic  8.67 us (7%)
  between operations  3.26 us (3%)
  local copies, waits for them, and re-layouts  1.44 us (1%)
    pallas_call x1, Pallas kernels, on_device(): pl.pallas_call(kernel, out_shape=(jax.ShapeDtypeStruct((3, col_width, use...  110 us
    add x1, other arithmetic, on_device(): user_factors + alpha_0 * start_r + alpha_1 * (mid_r + beta * start_r)  4.96 us
    sub x1, other arithmetic, on_device(): residual = mid_r - alpha_1 * (more * image_w + (beta - delta) * image_r)  3.71 us

profile of v5, /device:TPU:1, one launch (start us, length us, event | category | flops | bytes accessed | tf_op | source)
XLA Modules:
  0.0 123.7 jit_solution(10904844565869642070)
XLA Ops:
  0.6 0.0 copy-start
  1.3 110.4 %shard_map.77 = (f32[3,32,2048]{2,1,0:T(8,128)}, f32[8,128]{1,0:T(8,128)}) custom-call(s32[1]{0:T(128)S(6)} %copy.8.count_hbm, s32[72]{0:T(128)} %user_hbm.1, s32[72]{0:T(128)} %item_hbm.1, f32[32,2048]{1,0:T(8,128)} %users_in.1, bf16[32,8192]{1,0:T(8,128)(2,1)} %items_in.1, bf16[72,256,256]{2,1,0:T(8,128)(2,1)} %mask_ref.1), custom_call_target="tpu_custom_call" | custom-call | tf_op jit(solution)/shard_map/pallas_call | solution.py:529
  111.7 1.4 %fusion = (f32[1,1]{1,0:T(1,128)}, f32[1,1]{1,0:T(1,128)}, f32[1,1]{1,0:T(1,128)}, f32[1,1]{1,0:T(1,128)}, f32[1,1]{1,0:T(1,128)}) fusion(f32[8,128]{1,0:T(8,128)} %get-tuple-element.4), kind=kLoop, calls=%fused_computation.4 | loop fusion | bytes 40 | tf_op jit(solution)/shard_map/slice | solution.py:605
  115.0 0.0 copy-done
  115.1 5.0 %bitcast_add_fusion = f32[32,2048]{1,0:T(8,128)} fusion(f32[32,2048]{1,0:T(8,128)S(1)} %copy-done, f32[3,32,2048]{2,1,0:T(8,128)} %get-tuple-element.5, f32[]{:T(128)} %bitcast.2, f32[]{:T(128)} %bitcast.5, f32[]{:T(128)} %bitcast.3, f32[]{:T(128)} %bitcast.4, f32[]{:T(128)S(6)} %add_shard_map.3, f32[]{:T(128)} %bitcast), kind=kLoop, calls=%fused_computation | loop fusion | flops 720896 | bytes 1048600 | tf_op jit(solution)/shard_map/add | solution.py:608
  120.0 3.7 %subtract_bitcast_fusion = f32[32,2048]{1,0:T(8,128)} fusion(f32[3,32,2048]{2,1,0:T(8,128)} %get-tuple-element.5, f32[]{:T(128)} %bitcast.2, f32[]{:T(128)S(6)} %sub.19, f32[]{:T(128)} %bitcast.3, f32[]{:T(128)} %bitcast.4, f32[]{:T(128)S(6)} %add_shard_map.3), kind=kLoop, calls=%fused_computation.2 | loop fusion | flops 655360 | bytes 1048596 | tf_op jit(solution)/shard_map/sub | solution.py:609
Async XLA Ops:
  0.6 114.4 %copy-start = (f32[32,2048]{1,0:T(8,128)S(1)}, f32[32,2048]{1,0:T(8,128)}, u32[]{:S(2)}) copy-start(f32[32,2048]{1,0:T(8,128)} %users_in.1) | copy-start | bytes 786436

commit v6 on v5

--- a/solution.py
+++ b/solution.py
@@ -23,7 +23,7 @@
 PIECES = 4
 CHUNKS = 4
 NEAR = SLOTS - CAPACITY
-UNROLL = 36
+UNROLL = 24
 VMEM_BYTES = 56 * 1024 * 1024
 STARTS = (0, 2, 4, 6)
 PACK_AFTER = -0.5
@@ -39,7 +39,7 @@
 
 def kernel(
     count_hbm, user_hbm, item_hbm, users_in, items_in, mask_ref,
-    vectors_ref, scalars_ref,
+    solution_ref, residual_ref,
     count_ref, user_in, item_in, users_ref, items_ref, user_col, item_col, table, table_smem, ask, asked, asked_rows, asked_smem, ring_0, ring_1, ring_2, ring_3, far_0, far_1, far_2, far_3, plane_send,
     plane_recv_0, plane_recv_1, plane_recv_2, plane_recv_3, tiles, masks,
     users_send, users_recv, items_recv, gram_part, gram_recv, gram_piece, gram_all, gram,
@@ -360,7 +360,7 @@
     def sums_copy(at, peer, j, slot):
         return remote(sums_send.at[at], sums_recv.at[at, slot], s_send.at[at, j], s_recv.at[at, slot], peer(j))
 
-    def all_sums(products):
+    def all_sums(products, meanwhile):
         rows = [jnp.sum(p, axis=0, keepdims=True) for p in products]
         rows.append(jnp.zeros((8 - len(rows), 128), F32))
         total = jnp.sum(jnp.concatenate(rows, axis=0), axis=1, keepdims=True)
@@ -370,6 +370,8 @@
             sums_send[at] = total
             others(own, GROUP, lambda j: sums_copy(at, peer, j, own).start())
             sums_recv[at, own] = total
+            if at == 0:
+                meanwhile()
             others(own, GROUP, lambda j: sums_copy(at, peer, j, j).wait_recv())
             total = jnp.sum(sums_recv[at], axis=0)
         return [total[:, i : i + 1] for i in range(len(products))]
@@ -410,9 +412,8 @@
         others(col, n_cols, lambda j: user_copy(j, j).wait_recv())
         state_x[...] = users_recv[...].T
         mask_copy.wait()
-        others(own_a, GROUP, lambda j: gram_third(j, j).wait_recv())
         x_end(1)
-        state_r[...] = sparse_part(state_x[...], (0,), True) - dense_part(state_x[...])
+        state_r[...] = sparse_part(state_x[...], (0,), True)
 
     def gram_middle():
         x_end(0)
@@ -433,17 +434,18 @@
         events.append((start + span + PASS_AFTER, functools.partial(x_forward, piece)))
     events.append((STARTS[0] + span, gram_1))
     events.append((STARTS[0] + span + 2, gram_middle))
-    events.append((STARTS[-1] + span, gram_3))
+    events.append((STARTS[0] + span + 4, gram_3))
     events.append((STARTS[-1] + span, first_half))
     for _, event in sorted(events, key=lambda item: item[0]):
         event()
+    others(own_a, GROUP, lambda j: gram_third(j, j).wait_recv())
+    state_r[...] -= dense_part(state_x[...])
     x_end(2)
     x_end(3)
 
     state_r[...] += sparse_part(state_x[...], (1,), True)
     out_begin(0, state_r[...])
     image[...] = dense_part(state_r[...]) + CONFIDENCE * sparse_part(state_r[...], (0, 1), False)
-    out_begin(1, image[...])
 
     full = gram[...].reshape(128, 128)
     diagonal = lax.broadcasted_iota(jnp.int32, full.shape, 0) == lax.broadcasted_iota(jnp.int32, full.shape, 1)
@@ -451,7 +453,11 @@
     theta = 1.0 / (trace * (1.0 / 128) + RIDGE)
     state_d[...] = state_r[...] - theta * image[...]
     image_w = dense_part(state_d[...]) + CONFIDENCE * sparse_part(state_d[...], (0, 1), False)
-    out_begin(2, image_w)
+
+    def images_out():
+        out_begin(2, image_w)
+        out_begin(1, image[...])
+
     rr, rw, ww, ri, wi, rj, wj = all_sums(
         [
             state_r[...] * state_r[...],
@@ -461,7 +467,8 @@
             state_d[...] * image[...],
             state_r[...] * image_w,
             state_d[...] * image_w,
-        ]
+        ],
+        images_out,
     )
     delta = rw / (rr - rw)
     more = 1.0 + delta
@@ -482,13 +489,15 @@
     for block in range(blocks):
         lanes = pl.ds((block // 2) * 128, 128)
         for side in range(n_cols // 2):
+            start_r, image_r, image_d = [
+                interleave(out_recv[i, 2 * side, :, lanes], out_recv[i, 2 * side + 1, :, lanes], block % 2 == 1)
+                for i in range(3)
+            ]
             here = pl.ds(block * 256 + side * 128, 128)
-            for i in range(3):
-                vectors_ref[i, :, here] = interleave(
-                    out_recv[i, 2 * side, :, lanes], out_recv[i, 2 * side + 1, :, lanes], block % 2 == 1
-                )
-    for i, value in enumerate((theta, delta, alpha_0, alpha_1, beta)):
-        scalars_ref[i : i + 1, :] = jnp.broadcast_to(value, (1, 128))
+            mid_r = more * (start_r - theta * image_r) - delta * start_r
+            mid_x = users_ref[:, here] + alpha_0 * start_r
+            solution_ref[:, here] = mid_x + alpha_1 * (mid_r + beta * start_r)
+            residual_ref[:, here] = mid_r - alpha_1 * (more * image_d + (beta - delta) * image_r)
 
     others(own_p, PLANE, lambda j: ask_copy(j, own_p).wait_send())
     others(col, n_cols, lambda j: item_copy(j, col).wait_send())
@@ -526,12 +535,10 @@
     hbm = pl.BlockSpec(memory_space=pl.ANY)
     piece = width // GROUP
     dma = pltpu.SemaphoreType.DMA
-    vectors, scalars = pl.pallas_call(
+    out = jax.ShapeDtypeStruct((col_width, users), F32)
+    return pl.pallas_call(
         kernel,
-        out_shape=(
-            jax.ShapeDtypeStruct((3, col_width, users), F32),
-            jax.ShapeDtypeStruct((8, 128), F32),
-        ),
+        out_shape=(out, out),
         in_specs=[hbm] * 6,
         out_specs=(vmem, vmem),
         scratch_shapes=[
@@ -601,13 +608,6 @@
             collective_id=0, has_side_effects=True, vmem_limit_bytes=VMEM_BYTES
         ),
     )(tile_count, tile_user, tile_item, user_factors, item_factors, tile_mask)
-    start_r, image_r, image_w = vectors[0], vectors[1], vectors[2]
-    theta, delta, alpha_0, alpha_1, beta = [scalars[i, 0] for i in range(5)]
-    more = 1.0 + delta
-    mid_r = more * (start_r - theta * image_r) - delta * start_r
-    solution_field = user_factors + alpha_0 * start_r + alpha_1 * (mid_r + beta * start_r)
-    residual = mid_r - alpha_1 * (more * image_w + (beta - delta) * image_r)
-    return solution_field, residual
 
 
 def solution(mesh):

time: 124 us -> 110 us (0.89)
  other arithmetic: 8.67 us -> 0 us
  Pallas kernels: 110 us -> 106 us
  between operations: 3.26 us -> 1.29 us
  local copies, waits for them, and re-layouts: 1.44 us -> 3.34 us
    add x1 -> x0, other arithmetic: 4.96 us -> none  [on_device(): user_factors + alpha_0 * start_r + alpha_1 * (mid_r + beta * start_r)]
    pallas_call x1, Pallas kernels: 110 us -> 106 us  [on_device(): pl.pallas_call(kernel, out_shape=(out, out), in_specs=[hbm] * 6, out_spec...]
    sub x1 -> x0, other arithmetic: 3.71 us -> none  [on_device(): residual = mid_r - alpha_1 * (more * image_w + (beta - delta) * image_r)]
    unnamed x2, local copies, waits for them, and re-layouts: 0.01 us -> 3.34 us
    slice x1 -> x0, local copies, waits for them, and re-layouts: 1.44 us -> none  [on_device(): theta, delta, alpha_0, alpha_1, beta = [scalars[i, 0] for i in range(5)]]
where the time goes in v6:
time: 110 us
  Pallas kernels  106 us (96%)
  local copies, waits for them, and re-layouts  3.34 us (3%)
  between operations  1.29 us (1%)
    pallas_call x1, Pallas kernels, on_device(): pl.pallas_call(kernel, out_shape=(out, out), in_specs=[hbm] * 6, out_spec...  106 us
    unnamed x2, local copies, waits for them, and re-layouts  3.34 us

profile of v6, /device:TPU:1, one launch (start us, length us, event | category | flops | bytes accessed | tf_op | source)
XLA Modules:
  0.0 110.3 jit_solution(5407573734029587177)
XLA Ops:
  1.3 105.6 %shard_map.77 = (f32[32,2048]{1,0:T(8,128)}, f32[32,2048]{1,0:T(8,128)}) custom-call(s32[1]{0:T(128)S(6)} %copy.10.count_hbm, s32[72]{0:T(128)} %user_hbm.1, s32[72]{0:T(128)} %item_hbm.1, f32[32,2048]{1,0:T(8,128)} %users_in.1, bf16[32,8192]{1,0:T(8,128)(2,1)} %items_in.1, bf16[72,256,256]{2,1,0:T(8,128)(2,1)} %mask_ref.1), custom_call_target="tpu_custom_call" | custom-call | tf_op jit(solution)/shard_map/pallas_call | solution.py:539
  106.9 1.7 %copy.11 = f32[32,2048]{1,0:T(8,128)} copy(f32[32,2048]{1,0:T(8,128)} %get-tuple-element.4) | data formatting | bytes 524288
  108.6 1.7 %copy.12 = f32[32,2048]{1,0:T(8,128)} copy(f32[32,2048]{1,0:T(8,128)} %get-tuple-element.5) | data formatting | bytes 524288

commit v7 on v6

--- a/solution.py
+++ b/solution.py
@@ -370,8 +370,7 @@
             sums_send[at] = total
             others(own, GROUP, lambda j: sums_copy(at, peer, j, own).start())
             sums_recv[at, own] = total
-            if at == 0:
-                meanwhile()
+            meanwhile[at]()
             others(own, GROUP, lambda j: sums_copy(at, peer, j, j).wait_recv())
             total = jnp.sum(sums_recv[at], axis=0)
         return [total[:, i : i + 1] for i in range(len(products))]
@@ -458,6 +457,24 @@
         out_begin(2, image_w)
         out_begin(1, image[...])
 
+    def fetch_sent():
+        others(own_p, PLANE, lambda j: ask_copy(j, own_p).wait_send())
+        others(col, n_cols, lambda j: item_copy(j, col).wait_send())
+        others(col, n_cols, lambda j: user_copy(j, col).wait_send())
+        others(own_a, GROUP, lambda j: gram_first(j, own_a).wait_send())
+        others(own_b, GROUP, lambda j: gram_second(j, own_b).wait_send())
+        others(own_a, GROUP, lambda j: gram_third(j, own_a).wait_send())
+        for piece in range(PIECES):
+            for step in range(last_step + 1):
+                for way in range(2):
+                    for h in range(CHUNKS):
+                        if z_travels(step, way, h):
+                            z_copy(piece, way, step, h).wait_send()
+            for half in range(2):
+                others(own_p, PLANE, lambda j: plane_copy(piece, half, j, own_p).wait_send())
+            for kind, owner, peer in ((0, col, right), (1, col, right), (2, col, left), (3, col, left), (4, left, right), (5, right, left)):
+                x_copy(piece, kind, owner, peer).wait_send()
+
     rr, rw, ww, ri, wi, rj, wj = all_sums(
         [
             state_r[...] * state_r[...],
@@ -468,7 +485,7 @@
             state_r[...] * image_w,
             state_d[...] * image_w,
         ],
-        images_out,
+        (images_out, fetch_sent),
     )
     delta = rw / (rr - rw)
     more = 1.0 + delta
@@ -499,22 +516,6 @@
             solution_ref[:, here] = mid_x + alpha_1 * (mid_r + beta * start_r)
             residual_ref[:, here] = mid_r - alpha_1 * (more * image_d + (beta - delta) * image_r)
 
-    others(own_p, PLANE, lambda j: ask_copy(j, own_p).wait_send())
-    others(col, n_cols, lambda j: item_copy(j, col).wait_send())
-    others(col, n_cols, lambda j: user_copy(j, col).wait_send())
-    others(own_a, GROUP, lambda j: gram_first(j, own_a).wait_send())
-    others(own_b, GROUP, lambda j: gram_second(j, own_b).wait_send())
-    others(own_a, GROUP, lambda j: gram_third(j, own_a).wait_send())
-    for piece in range(PIECES):
-        for step in range(last_step + 1):
-            for way in range(2):
-                for h in range(CHUNKS):
-                    if z_travels(step, way, h):
-                        z_copy(piece, way, step, h).wait_send()
-        for half in range(2):
-            others(own_p, PLANE, lambda j: plane_copy(piece, half, j, own_p).wait_send())
-        for kind, owner, peer in ((0, col, right), (1, col, right), (2, col, left), (3, col, left), (4, left, right), (5, right, left)):
-            x_copy(piece, kind, owner, peer).wait_send()
     others(own_a, GROUP, lambda j: sums_copy(0, peer_a, j, own_a).wait_send())
     others(own_b, GROUP, lambda j: sums_copy(1, peer_b, j, own_b).wait_send())
     for index in range(3):

time: 110 us -> 109 us (level)
  Pallas kernels: 106 us -> 104 us
    pallas_call x1, Pallas kernels: 106 us -> 104 us  [on_device(): pl.pallas_call(kernel, out_shape=(out, out), in_specs=[hbm] * 6, out_spec...]
where the time goes in v7:
time: 109 us
  Pallas kernels  104 us (95%)
  local copies, waits for them, and re-layouts  3.34 us (3%)
  between operations  1.29 us (1%)
    pallas_call x1, Pallas kernels, on_device(): pl.pallas_call(kernel, out_shape=(out, out), in_specs=[hbm] * 6, out_spec...  104 us
    unnamed x2, local copies, waits for them, and re-layouts  3.34 us

profile of v7, /device:TPU:1, one launch (start us, length us, event | category | flops | bytes accessed | tf_op | source)
XLA Modules:
  0.0 108.6 jit_solution(6469686957366414795)
XLA Ops:
  1.3 104.0 %shard_map.77 = (f32[32,2048]{1,0:T(8,128)}, f32[32,2048]{1,0:T(8,128)}) custom-call(s32[1]{0:T(128)S(6)} %copy.10.count_hbm, s32[72]{0:T(128)} %user_hbm.1, s32[72]{0:T(128)} %item_hbm.1, f32[32,2048]{1,0:T(8,128)} %users_in.1, bf16[32,8192]{1,0:T(8,128)(2,1)} %items_in.1, bf16[72,256,256]{2,1,0:T(8,128)(2,1)} %mask_ref.1), custom_call_target="tpu_custom_call" | custom-call | tf_op jit(solution)/shard_map/pallas_call | solution.py:540
  105.3 1.7 %copy.11 = f32[32,2048]{1,0:T(8,128)} copy(f32[32,2048]{1,0:T(8,128)} %get-tuple-element.4) | data formatting | bytes 524288
  106.9 1.7 %copy.12 = f32[32,2048]{1,0:T(8,128)} copy(f32[32,2048]{1,0:T(8,128)} %get-tuple-element.5) | data formatting | bytes 524288
